TPU v7x, 32 devices: a whole 2x2x4 slice. The times are simulated.
32 devices in a mesh: dp: 8 (over z, x), mp: 4 (over y, core).
Axes of the slice: x: 2, y: 2, z: 4, core: 2. Of those that a mesh axis runs over, the one named last changes fastest.
Arguments:
- normed: bfloat16 [6144, 6144], P('dp', 'mp'), may hold values from -6 to 6
- pre_act: bfloat16 [6144, 24576], P('dp', 'mp'), may hold values from -6 to 6
- cotangent: bfloat16 [6144, 24576], P('dp', 'mp'), may hold values from -0.076171875 to 0.076171875
Outputs:
- up_grad: bfloat16 [6144, 24576], P('dp', 'mp')
All inputs are finite; a program needn't handle non-finite values.
Results may differ from a plain program's by a relative error of at most 0.012.
Values may be sent and summed in bfloat16 or wider, within the bound.
A program may use at most 256 MiB of HBM per device.

v0:
```python
import math

import jax
import jax.numpy as jnp
from jax import lax
from jax.sharding import PartitionSpec as P


def slope_of(pre_value):
    return 0.5 * (1.0 + lax.erf(pre_value / math.sqrt(2.0))) + pre_value * jnp.exp(
        -0.5 * pre_value * pre_value
    ) / math.sqrt(2.0 * math.pi)


def contract_rows(left, right):
    return lax.dot_general(
        left, right, (((0,), (0,)), ((), ())), preferred_element_type=jnp.float32
    )


def local(normed, pre_act, cotangent):
    gelu_slope = slope_of(pre_act.astype(jnp.float32))
    pre_grad = (cotangent.astype(jnp.float32) * gelu_slope).astype(jnp.bfloat16)
    gathered = lax.all_gather(normed, "mp", axis=1, tiled=True)
    return lax.psum_scatter(
        contract_rows(gathered, pre_grad).astype(jnp.bfloat16),
        "dp",
        scatter_dimension=0,
        tiled=True,
    )


def solution(mesh):
    return jax.shard_map(
        local,
        mesh=mesh,
        in_specs=(P("dp", "mp"), P("dp", "mp"), P("dp", "mp")),
        out_specs=P("dp", "mp"),
        check_vma=False,
    )
```

profile of v0, /device:TPU:0, one launch (start us, length us, event | category | flops | bytes accessed | tf_op | source)
XLA Modules:
  0.0 1347.5 jit_solution(4578799145566125637)
XLA Ops:
  6.5 0.0 all-gather.2.cloned.1.call-start
  6.5 0.7 all-gather.2.cloned.1.call-update
  7.3 0.0 reduce-scatter.2.cloned.1.call-start
  7.3 68.6 %all-gather.2.cloned.1.call-done = bf16[768,6144]{1,0:T(8,128)(2,1)} async-done(((bf16[768,1536]{1,0:T(8,128)(2,1)}), bf16[768,6144]{1,0:T(8,128)(2,1)}) %all-gather.2.cloned.1.call-update) | async-done | bytes 9437200 | tf_op jit(solution)/shard_map/all_gather | solution.py:24
  75.9 74.5 %convert_bitcast_fusion = bf16[6144,6144]{0,1:T(8,128)(2,1)} fusion(bf16[768,6144]{1,0:T(8,128)(2,1)} %all-gather.2.cloned.1.call-done, bf16[768,6144]{1,0:T(8,128)(2,1)} %param.4, bf16[768,6144]{1,0:T(8,128)(2,1)} %param.5), kind=kOutput, calls=%fused_computation | convolution fusion | flops 58076430336 | bytes 103809024 | tf_op jit(solution)/shard_map/dot_general | solution.py:16
  150.4 0.0 reduce-scatter.2.cloned.1.call-update
  150.5 1177.6 %reduce-scatter.2.cloned.1.call-done = bf16[768,6144]{0,1:T(8,128)(2,1)} async-done(((bf16[6144,6144]{0,1:T(8,128)(2,1)}), bf16[768,6144]{0,1:T(8,128)(2,1)}) %reduce-scatter.2.cloned.1.call-update) | async-done | bytes 9437200 | tf_op jit(solution)/shard_map/reduce_scatter | solution.py:25
  1328.0 12.6 copy.4
Async XLA Ops:
  6.5 69.4 %all-gather.2.cloned.1.call-start = ((), (), s32[]{:S(2)}) async-start(), calls=%async_computation.1 | async-start | bytes 11796480 | tf_op jit(solution)/shard_map/all_gather | solution.py:24
  7.3 1320.8 %reduce-scatter.2.cloned.1.call-start = ((), (), s32[]{:S(2)}) async-start(), calls=%async_computation.2 | async-start | bytes 84934656 | tf_op jit(solution)/shard_map/reduce_scatter | solution.py:25
Sparse Core Ops, SparseCore 0:
  8.9 66.9 all-gather.1
  150.6 1177.4 reduce-scatter.1
where the time goes:
time: 1350 us
  waiting for transfers between devices  1250 us (93%)
  matrix products  74.5 us (6%)
    reduce_scatter x1, waiting for transfers between devices, local(): lax.psum_scatter(contract_rows(gathered, pre_grad).astype(jnp.bfloat16),...  1180 us
    dot_general x1, matrix products, contract_rows(): lax.dot_general(left, right, (((0,), (0,)), ((), ())), preferred_element_...  74.5 us
    all_gather x1, waiting for transfers between devices, local(): gathered = lax.all_gather(normed, 'mp', axis=1, tiled=True)  68.6 us
  transfers between devices with their start and end apart: 2, of which 2 were waited for; matrix products, arithmetic and copies ran while one was open for 0% of the time, Pallas kernels for 0%

commit v1 on v0

v1 whole, which is shorter than its diff:
```python
import math

import jax
import jax.numpy as jnp
from jax import lax
from jax.sharding import PartitionSpec as P

CHUNKS = 8


def slope_of(pre_value):
    return 0.5 * (1.0 + lax.erf(pre_value / math.sqrt(2.0))) + pre_value * jnp.exp(
        -0.5 * pre_value * pre_value
    ) / math.sqrt(2.0 * math.pi)


def contract_rows(left, right):
    return lax.dot_general(
        left, right, (((0,), (0,)), ((), ())), preferred_element_type=jnp.float32
    )


def build(n_dp, n_mp):
    n_hi = n_dp // 4

    def dp_pairs(hi_step, lo_flip, x_flip):
        pairs = []
        for d in range(n_dp):
            hi, lo, x = d // 4, d // 2 % 2, d % 2
            pairs.append((d, ((hi + hi_step) % n_hi * 2 + (lo ^ lo_flip)) * 2 + (x ^ x_flip)))
        return pairs

    def move(value, hi_step, lo_flip, x_flip):
        return lax.ppermute(value, "dp", dp_pairs(hi_step, lo_flip, x_flip))

    def gather_left(normed):
        lo = lax.axis_index("dp") // 2 % 2
        tokens = normed.shape[0]
        x = lax.axis_index("dp") % 2
        if n_dp == 8 and n_mp == 4:
            rows = normed.shape[1] // 2
            pieces = []
            for flip in range(2):
                pairs = []
                for d in range(n_dp):
                    hi, low, xs = d // 4, d // 2 % 2, d % 2
                    for m in range(n_mp):
                        y, core = m // 2, m % 2
                        to_d = (hi * 2 + core) * 2 + (xs ^ flip)
                        pairs.append((d * n_mp + m, to_d * n_mp + y * 2 + low))
                part = lax.dynamic_slice(normed, (0, (x ^ flip) * rows), (tokens, rows))
                pieces.append(lax.ppermute(part, ("dp", "mp"), pairs))
            full = lax.all_gather(jnp.stack(pieces), "mp", axis=0)
            return [
                [
                    [
                        lax.dynamic_index_in_dim(full, hi * 2 + (lo ^ j), 0, keepdims=False)[k]
                        for hi in range(n_hi)
                    ]
                    for k in range(2)
                ]
                for j in range(2)
            ]
        full = lax.all_gather(normed, "mp", axis=1, tiled=True)
        full = full.reshape(tokens, n_hi, 2, 2, full.shape[1] // n_dp)
        found = []
        for j in range(2):
            found.append([])
            for k in range(2):
                part = lax.dynamic_index_in_dim(full, lo ^ j, 2, keepdims=False)
                part = lax.dynamic_index_in_dim(part, x ^ k, 2, keepdims=False)
                if j or k:
                    part = move(part, 0, j, k)
                found[j].append([part[:, hi] for hi in range(n_hi)])
        return found

    def local(normed, pre_act, cotangent):
        my_hi = lax.axis_index("dp") // 4
        left = gather_left(normed)
        order = [(0, 0), (0, 1), (1, 0), (1, 1)]
        stacked = jnp.stack([jnp.concatenate([left[j][k][hi] for j, k in order]) for hi in range(n_hi)])
        width = pre_act.shape[1] // CHUNKS
        out = jnp.zeros((stacked.shape[2], pre_act.shape[1]), jnp.bfloat16)
        for i in range(CHUNKS):
            cut = slice(i * width, (i + 1) * width)
            slope = slope_of(pre_act[:, cut].astype(jnp.float32))
            own = (cotangent[:, cut].astype(jnp.float32) * slope).astype(jnp.bfloat16)
            beside = move(own, 0, 1, 0)
            across = move(own, 0, 0, 1)
            both = move(beside, 0, 0, 1)
            right = jnp.concatenate([own, across, beside, both])

            def partial(step):
                return contract_rows(
                    lax.dynamic_index_in_dim(stacked, (my_hi + step) % n_hi, 0, keepdims=False), right
                )

            sent = [move(partial(step).astype(jnp.bfloat16), step, 0, 0) for step in range(1, n_hi)]
            total = partial(0)
            for term in sent:
                total = total + term.astype(jnp.float32)
            out = lax.dynamic_update_slice(out, total.astype(jnp.bfloat16), (0, i * width))
        return out

    return local


def solution(mesh):
    return jax.shard_map(
        build(mesh.shape["dp"], mesh.shape["mp"]),
        mesh=mesh,
        in_specs=(P("dp", "mp"), P("dp", "mp"), P("dp", "mp")),
        out_specs=P("dp", "mp"),
        check_vma=False,
    )
```

time: 1350 us -> 791 us (0.59)
  waiting for transfers between devices: 1250 us -> 606 us
  starting transfers between devices: 0.04 us -> 46.7 us
  matrix products: 74.5 us -> 92.5 us
  other arithmetic: 0 us -> 18 us
    reduce_scatter x1 -> x0, waiting for transfers between devices: 1180 us -> none  [local(): lax.psum_scatter(contract_rows(gathered, pre_grad).astype(jnp.bfloat16),...]
    ppermute x0 -> x34, waiting for transfers between devices: none -> 559 us  [the longest x32 533 us: move(): return lax.ppermute(value, 'dp', dp_pairs(hi_step, lo_flip, x_flip))]
    ppermute x0 -> x34, starting transfers between devices: none -> 46.7 us  [the longest x32 43 us: move(): return lax.ppermute(value, 'dp', dp_pairs(hi_step, lo_flip, x_flip))]
    all_gather x1, waiting for transfers between devices: 68.6 us -> 47 us  [gather_left(): full = lax.all_gather(jnp.stack(pieces), 'mp', axis=0)]
    dot_general x1 -> x16, matrix products: 74.5 us -> 92.5 us  [contract_rows(): lax.dot_general(left, right, (((0,), (0,)), ((), ())), preferred_element_...]
  transfers between devices with their start and end apart: 2 -> 35, of which waited for: 2 -> 25; matrix products, arithmetic and copies ran while one was open for 0% -> 14% of each run, Pallas kernels for 0% -> 0%
where the time goes in v1:
time: 791 us; the launch traced here: 787 us
  waiting for transfers between devices  606 us (77%)
  matrix products  92.5 us (12%)
  starting transfers between devices  46.7 us (6%)
  other arithmetic  18 us (2%)
  between operations  14.3 us (2%)
  local copies, waits for them, and re-layouts  9.22 us (1%)
    ppermute x32, waiting for transfers between devices, move(): return lax.ppermute(value, 'dp', dp_pairs(hi_step, lo_flip, x_flip))  533 us
    dot_general x16, matrix products, contract_rows(): lax.dot_general(left, right, (((0,), (0,)), ((), ())), preferred_element_...  92.5 us
    all_gather x1, waiting for transfers between devices, gather_left(): full = lax.all_gather(jnp.stack(pieces), 'mp', axis=0)  47 us
    ppermute x32, starting transfers between devices, move(): return lax.ppermute(value, 'dp', dp_pairs(hi_step, lo_flip, x_flip))  43 us
    ppermute x2, waiting for transfers between devices, gather_left(): pieces.append(lax.ppermute(part, ('dp', 'mp'), pairs))  26.1 us
  transfers between devices with their start and end apart: 35, of which 25 were waited for; matrix products, arithmetic and copies ran while one was open for 14% of the time, Pallas kernels for 0%

profile of v1, /device:TPU:0, one launch (start us, length us, event | category | flops | bytes accessed | tf_op | source)
XLA Modules:
  0.0 786.7 jit_solution(3393601903045595258)
XLA Ops:
  8.3 3.0 collective-permute-start.1
  12.1 26.1 %collective-permute-done.1 = bf16[768,768]{1,0:T(8,128)(2,1)S(1)} collective-permute-done((bf16[768,768]{1,0:T(8,128)(2,1)S(1)}, bf16[768,768]{1,0:T(8,128)(2,1)S(1)}, u32[]{:S(2)}, u32[]{:S(2)}) %collective-permute-start.1) | collective-permute-done | bytes 1179680 | tf_op jit(solution)/shard_map/ppermute | solution.py:52
  39.8 12.1 %fusion.60 = (bf16[768,768]{1,0:T(8,128)(2,1)S(1)}, bf16[768,768]{1,0:T(8,128)(2,1)}, bf16[768,768]{1,0:T(8,128)(2,1)}, bf16[768,768]{1,0:T(8,128)(2,1)}, bf16[7...) fusion(bf16[768,6144]{1,0:T(8,128)(2,1)} %param.4, ...), kind=kLoop, calls=%fused_computation.115 | loop fusion | flops 56623104 | bytes 28311552 | tf_op jit(solution)/shard_map/convert_element_type | solution.py:87
  51.9 2.6 collective-permute-start.3
  58.5 47.0 %all-gather.3.cloned.1.call-done = bf16[8,768,768]{2,1,0:T(8,128)(2,1)} async-done(((bf16[2,768,768]{2,1,0:T(8,128)(2,1)}), bf16[8,768,768]{2,1,0:T(8,128)(2,1)}) %all-gather.3.cloned.1.call-update) | async-done | bytes 9437200 | tf_op jit(solution)/shard_map/all_gather | solution.py:53
  105.4 4.4 dynamic-slice_bitcast_fusion.3
  115.6 16.3 %collective-permute-done.11 = bf16[768,768]{1,0:T(8,128)(2,1)} collective-permute-done((bf16[768,768]{1,0:T(8,128)(2,1)}, bf16[768,768]{1,0:T(8,128)(2,1)}, u32[]{:S(2)}, u32[]{:S(2)}) %collective-permute-start.11) | collective-permute-done | bytes 1179680 | tf_op jit(solution)/shard_map/ppermute | solution.py:34
  133.5 3.6 fusion.3
  140.4 23.8 %collective-permute-done.4 = bf16[768,768]{1,0:T(8,128)(2,1)S(1)} collective-permute-done((bf16[768,768]{1,0:T(8,128)(2,1)}, bf16[768,768]{1,0:T(8,128)(2,1)S(1)}, u32[]{:S(2)}, u32[]{:S(2)}) %collective-permute-start.4) | collective-permute-done | bytes 1179680 | tf_op jit(solution)/shard_map/ppermute | solution.py:34
  165.7 6.3 convolution_convert_fusion.7
  172.6 16.8 %collective-permute-done.14 = bf16[768,768]{1,0:T(8,128)(2,1)S(1)} collective-permute-done((bf16[768,768]{1,0:T(8,128)(2,1)}, bf16[768,768]{1,0:T(8,128)(2,1)S(1)}, u32[]{:S(2)}, u32[]{:S(2)}) %collective-permute-start.14) | collective-permute-done | bytes 1179680 | tf_op jit(solution)/shard_map/ppermute | solution.py:34
  191.0 23.7 %collective-permute-done.8 = bf16[768,768]{1,0:T(8,128)(2,1)S(1)} collective-permute-done((bf16[768,768]{1,0:T(8,128)(2,1)}, bf16[768,768]{1,0:T(8,128)(2,1)S(1)}, u32[]{:S(2)}, u32[]{:S(2)}) %collective-permute-start.8) | collective-permute-done | bytes 1179680 | tf_op jit(solution)/shard_map/ppermute | solution.py:34
  216.2 7.0 convolution_convert_fusion.6
  224.8 15.3 %collective-permute-done.12 = bf16[768,768]{1,0:T(8,128)(2,1)S(1)} collective-permute-done((bf16[768,768]{1,0:T(8,128)(2,1)}, bf16[768,768]{1,0:T(8,128)(2,1)S(1)}, u32[]{:S(2)}, u32[]{:S(2)}) %collective-permute-start.12) | collective-permute-done | bytes 1179680 | tf_op jit(solution)/shard_map/ppermute | solution.py:34
  241.5 6.6 convolution_convert_fusion.5
  248.1 17.2 %collective-permute-done.18 = bf16[768,768]{1,0:T(8,128)(2,1)S(1)} collective-permute-done((bf16[768,768]{1,0:T(8,128)(2,1)S(1)}, bf16[768,768]{1,0:T(8,128)(2,1)S(1)}, u32[]{:S(2)}, u32[]{:S(2)}) %collective-permute-start.18) | collective-permute-done | bytes 1179680 | tf_op jit(solution)/shard_map/ppermute | solution.py:34
  268.2 22.3 %collective-permute-done.16 = bf16[768,768]{1,0:T(8,128)(2,1)S(1)} collective-permute-done((bf16[768,768]{1,0:T(8,128)(2,1)S(1)}, bf16[768,768]{1,0:T(8,128)(2,1)S(1)}, u32[]{:S(2)}, u32[]{:S(2)}) %collective-permute-start.16) | collective-permute-done | bytes 1179680 | tf_op jit(solution)/shard_map/ppermute | solution.py:34
  292.0 6.7 convolution_convert_fusion.4
  299.4 16.4 %collective-permute-done.20 = bf16[768,768]{1,0:T(8,128)(2,1)S(1)} collective-permute-done((bf16[768,768]{1,0:T(8,128)(2,1)S(1)}, bf16[768,768]{1,0:T(8,128)(2,1)S(1)}, u32[]{:S(2)}, u32[]{:S(2)}) %collective-permute-start.20) | collective-permute-done | bytes 1179680 | tf_op jit(solution)/shard_map/ppermute | solution.py:34
  317.3 5.0 convolution_convert_fusion.3
  322.4 18.8 %collective-permute-done.22 = bf16[768,768]{1,0:T(8,128)(2,1)S(1)} collective-permute-done((bf16[768,768]{1,0:T(8,128)(2,1)S(1)}, bf16[768,768]{1,0:T(8,128)(2,1)S(1)}, u32[]{:S(2)}, u32[]{:S(2)}) %collective-permute-start.22) | collective-permute-done | bytes 1179680 | tf_op jit(solution)/shard_map/ppermute | solution.py:34
  343.2 23.2 %collective-permute-done.24 = bf16[768,768]{1,0:T(8,128)(2,1)S(1)} collective-permute-done((bf16[768,768]{1,0:T(8,128)(2,1)S(1)}, bf16[768,768]{1,0:T(8,128)(2,1)S(1)}, u32[]{:S(2)}, u32[]{:S(2)}) %collective-permute-start.24) | collective-permute-done | bytes 1179680 | tf_op jit(solution)/shard_map/ppermute | solution.py:34
  366.4 2.4 collective-permute-start.5
  368.8 5.0 convolution_convert_fusion.2
  373.8 17.9 %collective-permute-done.26 = bf16[768,768]{1,0:T(8,128)(2,1)S(1)} collective-permute-done((bf16[768,768]{1,0:T(8,128)(2,1)S(1)}, bf16[768,768]{1,0:T(8,128)(2,1)S(1)}, u32[]{:S(2)}, u32[]{:S(2)}) %collective-permute-start.26) | collective-permute-done | bytes 1179680 | tf_op jit(solution)/shard_map/ppermute | solution.py:34
  391.7 2.4 collective-permute-start.9
  394.1 22.9 %collective-permute-done.28 = bf16[768,768]{1,0:T(8,128)(2,1)S(1)} collective-permute-done((bf16[768,768]{1,0:T(8,128)(2,1)S(1)}, bf16[768,768]{1,0:T(8,128)(2,1)S(1)}, u32[]{:S(2)}, u32[]{:S(2)}) %collective-permute-start.28) | collective-permute-done | bytes 1179680 | tf_op jit(solution)/shard_map/ppermute | solution.py:34
  419.4 5.2 convolution_convert_fusion.1
  424.6 17.7 %collective-permute-done.30 = bf16[768,768]{1,0:T(8,128)(2,1)S(1)} collective-permute-done((bf16[768,768]{1,0:T(8,128)(2,1)S(1)}, bf16[768,768]{1,0:T(8,128)(2,1)S(1)}, u32[]{:S(2)}, u32[]{:S(2)}) %collective-permute-start.30) | collective-permute-done | bytes 1179680 | tf_op jit(solution)/shard_map/ppermute | solution.py:34
  444.7 22.2 %collective-permute-done.32 = bf16[768,768]{1,0:T(8,128)(2,1)S(1)} collective-permute-done((bf16[768,768]{1,0:T(8,128)(2,1)S(1)}, bf16[768,768]{1,0:T(8,128)(2,1)S(1)}, u32[]{:S(2)}, u32[]{:S(2)}) %collective-permute-start.32) | collective-permute-done | bytes 1179680 | tf_op jit(solution)/shard_map/ppermute | solution.py:34
  469.3 5.0 convolution_convert_fusion
  474.3 47.2 %collective-permute-done.5 = bf16[768,768]{1,0:T(8,128)(2,1)S(1)} collective-permute-done((bf16[768,768]{1,0:T(8,128)(2,1)S(1)}, bf16[768,768]{1,0:T(8,128)(2,1)S(1)}, u32[]{:S(2)}, u32[]{:S(2)}) %collective-permute-start.5) | collective-permute-done | bytes 1179680 | tf_op jit(solution)/shard_map/ppermute | solution.py:34
  521.5 6.3 add_convert_fusion.7
  527.7 2.4 dynamic_update_slice.24
  530.2 41.9 %collective-permute-done.9 = bf16[768,768]{1,0:T(8,128)(2,1)} collective-permute-done((bf16[768,768]{1,0:T(8,128)(2,1)}, bf16[768,768]{1,0:T(8,128)(2,1)}, u32[]{:S(2)}, u32[]{:S(2)}) %collective-permute-start.9) | collective-permute-done | bytes 1179680 | tf_op jit(solution)/shard_map/ppermute | solution.py:34
  572.1 6.9 fusion.68
  579.0 43.6 %collective-permute-done.13 = bf16[768,768]{1,0:T(8,128)(2,1)} collective-permute-done((bf16[768,768]{1,0:T(8,128)(2,1)}, bf16[768,768]{1,0:T(8,128)(2,1)}, u32[]{:S(2)}, u32[]{:S(2)}) %collective-permute-start.13) | collective-permute-done | bytes 1179680 | tf_op jit(solution)/shard_map/ppermute | solution.py:34
  622.7 5.9 fusion.69
  628.7 44.5 %collective-permute-done.17 = bf16[768,768]{1,0:T(8,128)(2,1)} collective-permute-done((bf16[768,768]{1,0:T(8,128)(2,1)}, bf16[768,768]{1,0:T(8,128)(2,1)}, u32[]{:S(2)}, u32[]{:S(2)}) %collective-permute-start.17) | collective-permute-done | bytes 1179680 | tf_op jit(solution)/shard_map/ppermute | solution.py:34
  673.2 5.6 fusion.70
  678.9 19.6 %collective-permute-done.21 = bf16[768,768]{1,0:T(8,128)(2,1)} collective-permute-done((bf16[768,768]{1,0:T(8,128)(2,1)}, bf16[768,768]{1,0:T(8,128)(2,1)}, u32[]{:S(2)}, u32[]{:S(2)}) %collective-permute-start.21) | collective-permute-done | bytes 1179680 | tf_op jit(solution)/shard_map/ppermute | solution.py:34
  698.5 5.5 fusion.71
  704.1 19.7 %collective-permute-done.25 = bf16[768,768]{1,0:T(8,128)(2,1)} collective-permute-done((bf16[768,768]{1,0:T(8,128)(2,1)}, bf16[768,768]{1,0:T(8,128)(2,1)}, u32[]{:S(2)}, u32[]{:S(2)}) %collective-permute-start.25) | collective-permute-done | bytes 1179680 | tf_op jit(solution)/shard_map/ppermute | solution.py:34
  723.8 5.2 fusion.72
  729.1 19.9 %collective-permute-done.29 = bf16[768,768]{1,0:T(8,128)(2,1)S(1)} collective-permute-done((bf16[768,768]{1,0:T(8,128)(2,1)}, bf16[768,768]{1,0:T(8,128)(2,1)S(1)}, u32[]{:S(2)}, u32[]{:S(2)}) %collective-permute-start.29) | collective-permute-done | bytes 1179680 | tf_op jit(solution)/shard_map/ppermute | solution.py:34
  749.0 4.0 fusion.73
  753.0 20.2 %collective-permute-done.33 = bf16[768,768]{1,0:T(8,128)(2,1)} collective-permute-done((bf16[768,768]{1,0:T(8,128)(2,1)S(1)}, bf16[768,768]{1,0:T(8,128)(2,1)}, u32[]{:S(2)}, u32[]{:S(2)}) %collective-permute-start.33) | collective-permute-done | bytes 1179680 | tf_op jit(solution)/shard_map/ppermute | solution.py:34
  773.3 6.1 fusion.74
  (148 shorter events, 42.9 us)
Async XLA Ops:
  6.5 98.9 %all-gather.3.cloned.1.call-start = ((), (), s32[]{:S(2)}) async-start(), calls=%async_computation | async-start | bytes 11796480 | tf_op jit(solution)/shard_map/all_gather | solution.py:53
  8.3 29.8 %collective-permute-start.1 = (bf16[768,768]{1,0:T(8,128)(2,1)S(1)}, bf16[768,768]{1,0:T(8,128)(2,1)S(1)}, u32[]{:S(2)}, u32[]{:S(2)}) collective-permute-start(bf16[768,768]{1,0:T(8,128)(2,1)S(1)} %get-tuple-element.24), channel_id=1, source_target_pairs={{0,4},{1,12},{2,6},{3,14},{4,0},{5,8},{6,2},{7,10},{8,5},{9,13},{1... | collective-permute-start | bytes 3538952 | tf_op jit(solution)/shard_map/ppermute | solution.py:52
  11.3 26.8 %collective-permute-start = (bf16[768,768]{1,0:T(8,128)(2,1)S(1)}, bf16[768,768]{1,0:T(8,128)(2,1)S(1)}, u32[]{:S(2)}, u32[]{:S(2)}) collective-permute-start(bf16[768,768]{1,0:T(8,128)(2,1)S(1)} %get-tuple-element.23), channel_id=1, source_target_pairs={{0,0},{1,8},{2,2},{3,10},{4,4},{5,12},{6,6},{7,14},{8,1},{9,9},{10... | collective-permute-start | bytes 3538952 | tf_op jit(solution)/shard_map/ppermute | solution.py:52
  51.9 58.0 %collective-permute-start.3 = (bf16[768,768]{1,0:T(8,128)(2,1)S(1)}, bf16[768,768]{1,0:T(8,128)(2,1)}, u32[]{:S(2)}, u32[]{:S(2)}) collective-permute-start(bf16[768,768]{1,0:T(8,128)(2,1)S(1)} %get-tuple-element.11), channel_id=1, source_target_pairs={{0,8},{4,12},{8,0},{12,4},{16,24},{20,28},{24,16},{28,20},{1,9},{5... | collective-permute-start | bytes 3538952 | tf_op jit(solution)/shard_map/ppermute | solution.py:34
  54.4 56.9 %collective-permute-start.2 = (bf16[768,768]{1,0:T(8,128)(2,1)S(1)}, bf16[768,768]{1,0:T(8,128)(2,1)S(1)}, u32[]{:S(2)}, u32[]{:S(2)}) collective-permute-start(bf16[768,768]{1,0:T(8,128)(2,1)S(1)} %get-tuple-element.11), channel_id=1, source_target_pairs={{0,4},{4,0},{8,12},{12,8},{16,20},{20,16},{24,28},{28,24},{1,5},{5... | collective-permute-start | bytes 3538952 | tf_op jit(solution)/shard_map/ppermute | solution.py:34
  55.0 58.1 %collective-permute-start.7 = (bf16[768,768]{1,0:T(8,128)(2,1)}, bf16[768,768]{1,0:T(8,128)(2,1)}, u32[]{:S(2)}, u32[]{:S(2)}) collective-permute-start(bf16[768,768]{1,0:T(8,128)(2,1)} %get-tuple-element.10), channel_id=1, source_target_pairs={{0,8},{4,12},{8,0},{12,4},{16,24},{20,28},{24,16},{28,20},{1,9},{5... | collective-permute-start | bytes 3538952 | tf_op jit(solution)/shard_map/ppermute | solution.py:34
  56.0 58.6 %collective-permute-start.6 = (bf16[768,768]{1,0:T(8,128)(2,1)}, bf16[768,768]{1,0:T(8,128)(2,1)}, u32[]{:S(2)}, u32[]{:S(2)}) collective-permute-start(bf16[768,768]{1,0:T(8,128)(2,1)} %get-tuple-element.10), channel_id=1, source_target_pairs={{0,4},{4,0},{8,12},{12,8},{16,20},{20,16},{24,28},{28,24},{1,5},{5... | collective-permute-start | bytes 3538952 | tf_op jit(solution)/shard_map/ppermute | solution.py:34
  56.5 75.3 %collective-permute-start.11 = (bf16[768,768]{1,0:T(8,128)(2,1)}, bf16[768,768]{1,0:T(8,128)(2,1)}, u32[]{:S(2)}, u32[]{:S(2)}) collective-permute-start(bf16[768,768]{1,0:T(8,128)(2,1)} %get-tuple-element.9), channel_id=1, source_target_pairs={{0,8},{4,12},{8,0},{12,4},{16,24},{20,28},{24,16},{28,20},{1,9},{5... | collective-permute-start | bytes 3538952 | tf_op jit(solution)/shard_map/ppermute | solution.py:34
  109.8 29.1 %collective-permute-start.10 = (bf16[768,768]{1,0:T(8,128)(2,1)}, bf16[768,768]{1,0:T(8,128)(2,1)S(1)}, u32[]{:S(2)}, u32[]{:S(2)}) collective-permute-start(bf16[768,768]{1,0:T(8,128)(2,1)} %get-tuple-element.9), channel_id=1, source_target_pairs={{0,4},{4,0},{8,12},{12,8},{16,20},{20,16},{24,28},{28,24},{1,5},{5... | collective-permute-start | bytes 3538952 | tf_op jit(solution)/shard_map/ppermute | solution.py:34
  111.4 52.8 %collective-permute-start.4 = (bf16[768,768]{1,0:T(8,128)(2,1)}, bf16[768,768]{1,0:T(8,128)(2,1)S(1)}, u32[]{:S(2)}, u32[]{:S(2)}) collective-permute-start(bf16[768,768]{1,0:T(8,128)(2,1)} %collective-permute-done.3), channel_id=1, source_target_pairs={{0,4},{4,0},{8,12},{12,8},{16,20},{20,16},{24,28},{28,24},{1,5},{5... | collective-permute-start | bytes 3538952 | tf_op jit(solution)/shard_map/ppermute | solution.py:34
  113.0 59.0 %collective-permute-start.15 = (bf16[768,768]{1,0:T(8,128)(2,1)}, bf16[768,768]{1,0:T(8,128)(2,1)S(1)}, u32[]{:S(2)}, u32[]{:S(2)}) collective-permute-start(bf16[768,768]{1,0:T(8,128)(2,1)} %get-tuple-element.8), channel_id=1, source_target_pairs={{0,8},{4,12},{8,0},{12,4},{16,24},{20,28},{24,16},{28,20},{1,9},{5... | collective-permute-start | bytes 3538952 | tf_op jit(solution)/shard_map/ppermute | solution.py:34
  114.6 74.9 %collective-permute-start.14 = (bf16[768,768]{1,0:T(8,128)(2,1)}, bf16[768,768]{1,0:T(8,128)(2,1)S(1)}, u32[]{:S(2)}, u32[]{:S(2)}) collective-permute-start(bf16[768,768]{1,0:T(8,128)(2,1)} %get-tuple-element.8), channel_id=1, source_target_pairs={{0,4},{4,0},{8,12},{12,8},{16,20},{20,16},{24,28},{28,24},{1,5},{5... | collective-permute-start | bytes 3538952 | tf_op jit(solution)/shard_map/ppermute | solution.py:34
  131.9 82.9 %collective-permute-start.8 = (bf16[768,768]{1,0:T(8,128)(2,1)}, bf16[768,768]{1,0:T(8,128)(2,1)S(1)}, u32[]{:S(2)}, u32[]{:S(2)}) collective-permute-start(bf16[768,768]{1,0:T(8,128)(2,1)} %collective-permute-done.7), channel_id=1, source_target_pairs={{0,4},{4,0},{8,12},{12,8},{16,20},{20,16},{24,28},{28,24},{1,5},{5... | collective-permute-start | bytes 3538952 | tf_op jit(solution)/shard_map/ppermute | solution.py:34
  138.9 84.3 %collective-permute-start.19 = (bf16[768,768]{1,0:T(8,128)(2,1)S(1)}, bf16[768,768]{1,0:T(8,128)(2,1)S(1)}, u32[]{:S(2)}, u32[]{:S(2)}) collective-permute-start(bf16[768,768]{1,0:T(8,128)(2,1)S(1)} %copy-done.5), channel_id=1, source_target_pairs={{0,8},{4,12},{8,0},{12,4},{16,24},{20,28},{24,16},{28,20},{1,9},{5... | collective-permute-start | bytes 3538952 | tf_op jit(solution)/shard_map/ppermute | solution.py:34
  164.2 75.8 %collective-permute-start.12 = (bf16[768,768]{1,0:T(8,128)(2,1)}, bf16[768,768]{1,0:T(8,128)(2,1)S(1)}, u32[]{:S(2)}, u32[]{:S(2)}) collective-permute-start(bf16[768,768]{1,0:T(8,128)(2,1)} %collective-permute-done.11), channel_id=1, source_target_pairs={{0,4},{4,0},{8,12},{12,8},{16,20},{20,16},{24,28},{28,24},{1,5},{5... | collective-permute-start | bytes 3538952 | tf_op jit(solution)/shard_map/ppermute | solution.py:34
  172.0 120.0 %copy-start.14 = (bf16[768,768]{1,0:T(8,128)(2,1)}, bf16[768,768]{1,0:T(8,128)(2,1)S(1)}, u32[]{:S(2)}) copy-start(bf16[768,768]{1,0:T(8,128)(2,1)S(1)} %collective-permute-done.15) | copy-start | bytes 3538948
  172.0 93.3 %collective-permute-start.18 = (bf16[768,768]{1,0:T(8,128)(2,1)S(1)}, bf16[768,768]{1,0:T(8,128)(2,1)S(1)}, u32[]{:S(2)}, u32[]{:S(2)}) collective-permute-start(bf16[768,768]{1,0:T(8,128)(2,1)S(1)} %copy-done.5), channel_id=1, source_target_pairs={{0,4},{4,0},{8,12},{12,8},{16,20},{20,16},{24,28},{28,24},{1,5},{5... | collective-permute-start | bytes 3538952 | tf_op jit(solution)/shard_map/ppermute | solution.py:34
  189.5 102.6 %copy-start.16 = (bf16[768,768]{1,0:T(8,128)(2,1)}, bf16[768,768]{1,0:T(8,128)(2,1)S(1)}, u32[]{:S(2)}) copy-start(bf16[768,768]{1,0:T(8,128)(2,1)S(1)} %collective-permute-done.14) | copy-start | bytes 3538948
  189.5 77.3 %collective-permute-start.23 = (bf16[768,768]{1,0:T(8,128)(2,1)S(1)}, bf16[768,768]{1,0:T(8,128)(2,1)S(1)}, u32[]{:S(2)}, u32[]{:S(2)}) collective-permute-start(bf16[768,768]{1,0:T(8,128)(2,1)S(1)} %copy-done.3), channel_id=1, source_target_pairs={{0,8},{4,12},{8,0},{12,4},{16,24},{20,28},{24,16},{28,20},{1,9},{5... | collective-permute-start | bytes 3538952 | tf_op jit(solution)/shard_map/ppermute | solution.py:34
  214.7 75.8 %collective-permute-start.16 = (bf16[768,768]{1,0:T(8,128)(2,1)S(1)}, bf16[768,768]{1,0:T(8,128)(2,1)S(1)}, u32[]{:S(2)}, u32[]{:S(2)}) collective-permute-start(bf16[768,768]{1,0:T(8,128)(2,1)S(1)} %collective-permute-done.15), channel_id=1, source_target_pairs={{0,4},{4,0},{8,12},{12,8},{16,20},{20,16},{24,28},{28,24},{1,5},{5... | collective-permute-start | bytes 3538952 | tf_op jit(solution)/shard_map/ppermute | solution.py:34
  223.2 94.1 %copy-start.18 = (bf16[768,768]{1,0:T(8,128)(2,1)}, bf16[768,768]{1,0:T(8,128)(2,1)S(1)}, u32[]{:S(2)}) copy-start(bf16[768,768]{1,0:T(8,128)(2,1)S(1)} %collective-permute-done.19) | copy-start | bytes 3538948
  223.2 75.6 %collective-permute-start.27 = (bf16[768,768]{1,0:T(8,128)(2,1)S(1)}, bf16[768,768]{1,0:T(8,128)(2,1)S(1)}, u32[]{:S(2)}, u32[]{:S(2)}) collective-permute-start(bf16[768,768]{1,0:T(8,128)(2,1)S(1)} %copy-done.1), channel_id=1, source_target_pairs={{0,8},{4,12},{8,0},{12,4},{16,24},{20,28},{24,16},{28,20},{1,9},{5... | collective-permute-start | bytes 3538952 | tf_op jit(solution)/shard_map/ppermute | solution.py:34
  240.0 75.8 %collective-permute-start.20 = (bf16[768,768]{1,0:T(8,128)(2,1)S(1)}, bf16[768,768]{1,0:T(8,128)(2,1)S(1)}, u32[]{:S(2)}, u32[]{:S(2)}) collective-permute-start(bf16[768,768]{1,0:T(8,128)(2,1)S(1)} %collective-permute-done.19), channel_id=1, source_target_pairs={{0,4},{4,0},{8,12},{12,8},{16,20},{20,16},{24,28},{28,24},{1,5},{5... | collective-permute-start | bytes 3538952 | tf_op jit(solution)/shard_map/ppermute | solution.py:34
  265.3 75.8 %collective-permute-start.22 = (bf16[768,768]{1,0:T(8,128)(2,1)S(1)}, bf16[768,768]{1,0:T(8,128)(2,1)S(1)}, u32[]{:S(2)}, u32[]{:S(2)}) collective-permute-start(bf16[768,768]{1,0:T(8,128)(2,1)S(1)} %copy-done.3), channel_id=1, source_target_pairs={{0,4},{4,0},{8,12},{12,8},{16,20},{20,16},{24,28},{28,24},{1,5},{5... | collective-permute-start | bytes 3538952 | tf_op jit(solution)/shard_map/ppermute | solution.py:34
  266.8 102.1 %copy-start.22 = (bf16[768,768]{1,0:T(8,128)(2,1)}, bf16[768,768]{1,0:T(8,128)(2,1)S(1)}, u32[]{:S(2)}) copy-start(bf16[768,768]{1,0:T(8,128)(2,1)S(1)} %collective-permute-done.23) | copy-start | bytes 3538948
  266.8 75.8 %collective-permute-start.31 = (bf16[768,768]{1,0:T(8,128)(2,1)S(1)}, bf16[768,768]{1,0:T(8,128)(2,1)S(1)}, u32[]{:S(2)}, u32[]{:S(2)}) collective-permute-start(bf16[768,768]{1,0:T(8,128)(2,1)S(1)} %get-tuple-element.5), channel_id=1, source_target_pairs={{0,8},{4,12},{8,0},{12,4},{16,24},{20,28},{24,16},{28,20},{1,9},{5... | collective-permute-start | bytes 3538952 | tf_op jit(solution)/shard_map/ppermute | solution.py:34
  290.6 75.8 %collective-permute-start.24 = (bf16[768,768]{1,0:T(8,128)(2,1)S(1)}, bf16[768,768]{1,0:T(8,128)(2,1)S(1)}, u32[]{:S(2)}, u32[]{:S(2)}) collective-permute-start(bf16[768,768]{1,0:T(8,128)(2,1)S(1)} %collective-permute-done.23), channel_id=1, source_target_pairs={{0,4},{4,0},{8,12},{12,8},{16,20},{20,16},{24,28},{28,24},{1,5},{5... | collective-permute-start | bytes 3538952 | tf_op jit(solution)/shard_map/ppermute | solution.py:34
  298.8 120.6 %copy-start.26 = (bf16[768,768]{1,0:T(8,128)(2,1)}, bf16[768,768]{1,0:T(8,128)(2,1)S(1)}, u32[]{:S(2)}) copy-start(bf16[768,768]{1,0:T(8,128)(2,1)S(1)} %collective-permute-done.27) | copy-start | bytes 3538948
  298.8 92.9 %collective-permute-start.26 = (bf16[768,768]{1,0:T(8,128)(2,1)S(1)}, bf16[768,768]{1,0:T(8,128)(2,1)S(1)}, u32[]{:S(2)}, u32[]{:S(2)}) collective-permute-start(bf16[768,768]{1,0:T(8,128)(2,1)S(1)} %copy-done.1), channel_id=1, source_target_pairs={{0,4},{4,0},{8,12},{12,8},{16,20},{20,16},{24,28},{28,24},{1,5},{5... | collective-permute-start | bytes 3538952 | tf_op jit(solution)/shard_map/ppermute | solution.py:34
  315.9 101.1 %collective-permute-start.28 = (bf16[768,768]{1,0:T(8,128)(2,1)S(1)}, bf16[768,768]{1,0:T(8,128)(2,1)S(1)}, u32[]{:S(2)}, u32[]{:S(2)}) collective-permute-start(bf16[768,768]{1,0:T(8,128)(2,1)S(1)} %collective-permute-done.27), channel_id=1, source_target_pairs={{0,4},{4,0},{8,12},{12,8},{16,20},{20,16},{24,28},{28,24},{1,5},{5... | collective-permute-start | bytes 3538952 | tf_op jit(solution)/shard_map/ppermute | solution.py:34
  341.1 101.1 %collective-permute-start.30 = (bf16[768,768]{1,0:T(8,128)(2,1)S(1)}, bf16[768,768]{1,0:T(8,128)(2,1)S(1)}, u32[]{:S(2)}, u32[]{:S(2)}) collective-permute-start(bf16[768,768]{1,0:T(8,128)(2,1)S(1)} %get-tuple-element.5), channel_id=1, source_target_pairs={{0,4},{4,0},{8,12},{12,8},{16,20},{20,16},{24,28},{28,24},{1,5},{5... | collective-permute-start | bytes 3538952 | tf_op jit(solution)/shard_map/ppermute | solution.py:34
  342.6 126.7 %copy-start.29 = (bf16[768,768]{1,0:T(8,128)(2,1)}, bf16[768,768]{1,0:T(8,128)(2,1)S(1)}, u32[]{:S(2)}) copy-start(bf16[768,768]{1,0:T(8,128)(2,1)S(1)} %collective-permute-done.31) | copy-start | bytes 3538948
  342.6 124.3 %collective-permute-start.32 = (bf16[768,768]{1,0:T(8,128)(2,1)S(1)}, bf16[768,768]{1,0:T(8,128)(2,1)S(1)}, u32[]{:S(2)}, u32[]{:S(2)}) collective-permute-start(bf16[768,768]{1,0:T(8,128)(2,1)S(1)} %collective-permute-done.31), channel_id=1, source_target_pairs={{0,4},{4,0},{8,12},{12,8},{16,20},{20,16},{24,28},{28,24},{1,5},{5... | collective-permute-start | bytes 3538952 | tf_op jit(solution)/shard_map/ppermute | solution.py:34
  366.4 155.0 %collective-permute-start.5 = (bf16[768,768]{1,0:T(8,128)(2,1)S(1)}, bf16[768,768]{1,0:T(8,128)(2,1)S(1)}, u32[]{:S(2)}, u32[]{:S(2)}) collective-permute-start(bf16[768,768]{1,0:T(8,128)(2,1)S(1)} %copy-done.49), channel_id=1, source_target_pairs={{0,16},{4,20},{8,24},{12,28},{16,0},{20,4},{24,8},{28,12},{1,17},{... | collective-permute-start | bytes 3538952 | tf_op jit(solution)/shard_map/ppermute | solution.py:34
  391.7 180.4 %collective-permute-start.9 = (bf16[768,768]{1,0:T(8,128)(2,1)}, bf16[768,768]{1,0:T(8,128)(2,1)}, u32[]{:S(2)}, u32[]{:S(2)}) collective-permute-start(bf16[768,768]{1,0:T(8,128)(2,1)} %convolution_convert_fusion.6), channel_id=1, source_target_pairs={{0,16},{4,20},{8,24},{12,28},{16,0},{20,4},{24,8},{28,12},{1,17},{... | collective-permute-start | bytes 3538952 | tf_op jit(solution)/shard_map/ppermute | solution.py:34
  417.0 205.7 %collective-permute-start.13 = (bf16[768,768]{1,0:T(8,128)(2,1)}, bf16[768,768]{1,0:T(8,128)(2,1)}, u32[]{:S(2)}, u32[]{:S(2)}) collective-permute-start(bf16[768,768]{1,0:T(8,128)(2,1)} %convolution_convert_fusion.5), channel_id=1, source_target_pairs={{0,16},{4,20},{8,24},{12,28},{16,0},{20,4},{24,8},{28,12},{1,17},{... | collective-permute-start | bytes 3538952 | tf_op jit(solution)/shard_map/ppermute | solution.py:34
  424.6 96.9 %copy-start.21 = (bf16[768,768]{1,0:T(8,128)(2,1)S(1)}, bf16[768,768]{1,0:T(8,128)(2,1)}, u32[]{:S(2)}) copy-start(bf16[768,768]{1,0:T(8,128)(2,1)} %copy-done.20) | copy-start | bytes 3538948
  442.3 231.0 %collective-permute-start.17 = (bf16[768,768]{1,0:T(8,128)(2,1)}, bf16[768,768]{1,0:T(8,128)(2,1)}, u32[]{:S(2)}, u32[]{:S(2)}) collective-permute-start(bf16[768,768]{1,0:T(8,128)(2,1)} %convolution_convert_fusion.4), channel_id=1, source_target_pairs={{0,16},{4,20},{8,24},{12,28},{16,0},{20,4},{24,8},{28,12},{1,17},{... | collective-permute-start | bytes 3538952 | tf_op jit(solution)/shard_map/ppermute | solution.py:34
  466.9 231.6 %collective-permute-start.21 = (bf16[768,768]{1,0:T(8,128)(2,1)}, bf16[768,768]{1,0:T(8,128)(2,1)}, u32[]{:S(2)}, u32[]{:S(2)}) collective-permute-start(bf16[768,768]{1,0:T(8,128)(2,1)} %convolution_convert_fusion.3), channel_id=1, source_target_pairs={{0,16},{4,20},{8,24},{12,28},{16,0},{20,4},{24,8},{28,12},{1,17},{... | collective-permute-start | bytes 3538952 | tf_op jit(solution)/shard_map/ppermute | solution.py:34
  521.4 202.3 %collective-permute-start.25 = (bf16[768,768]{1,0:T(8,128)(2,1)}, bf16[768,768]{1,0:T(8,128)(2,1)}, u32[]{:S(2)}, u32[]{:S(2)}) collective-permute-start(bf16[768,768]{1,0:T(8,128)(2,1)} %convolution_convert_fusion.2), channel_id=1, source_target_pairs={{0,16},{4,20},{8,24},{12,28},{16,0},{20,4},{24,8},{28,12},{1,17},{... | collective-permute-start | bytes 3538952 | tf_op jit(solution)/shard_map/ppermute | solution.py:34
  530.2 92.5 %copy-start.50 = (bf16[768,768]{1,0:T(8,128)(2,1)S(1)}, bf16[768,768]{1,0:T(8,128)(2,1)}, u32[]{:S(2)}) copy-start(bf16[768,768]{1,0:T(8,128)(2,1)} %convolution_convert_fusion) | copy-start | bytes 3538948
  530.2 92.5 %copy-start.13 = (bf16[768,768]{1,0:T(8,128)(2,1)S(1)}, bf16[768,768]{1,0:T(8,128)(2,1)}, u32[]{:S(2)}) copy-start(bf16[768,768]{1,0:T(8,128)(2,1)} %copy-done.11) | copy-start | bytes 3538948
  530.2 92.5 %copy-start.32 = (bf16[768,768]{1,0:T(8,128)(2,1)S(1)}, bf16[768,768]{1,0:T(8,128)(2,1)}, u32[]{:S(2)}) copy-start(bf16[768,768]{1,0:T(8,128)(2,1)} %copy-done.31) | copy-start | bytes 3538948
  572.1 176.9 %collective-permute-start.29 = (bf16[768,768]{1,0:T(8,128)(2,1)}, bf16[768,768]{1,0:T(8,128)(2,1)S(1)}, u32[]{:S(2)}, u32[]{:S(2)}) collective-permute-start(bf16[768,768]{1,0:T(8,128)(2,1)} %convolution_convert_fusion.1), channel_id=1, source_target_pairs={{0,16},{4,20},{8,24},{12,28},{16,0},{20,4},{24,8},{28,12},{1,17},{... | collective-permute-start | bytes 3538952 | tf_op jit(solution)/shard_map/ppermute | solution.py:34
  579.0 94.2 %copy-start.15 = (bf16[768,768]{1,0:T(8,128)(2,1)S(1)}, bf16[768,768]{1,0:T(8,128)(2,1)}, u32[]{:S(2)}) copy-start(bf16[768,768]{1,0:T(8,128)(2,1)} %copy-done.14) | copy-start | bytes 3538948
  579.0 94.2 %copy-start.17 = (bf16[768,768]{1,0:T(8,128)(2,1)S(1)}, bf16[768,768]{1,0:T(8,128)(2,1)}, u32[]{:S(2)}) copy-start(bf16[768,768]{1,0:T(8,128)(2,1)} %copy-done.16) | copy-start | bytes 3538948
  579.0 94.2 %copy-start.34 = (bf16[768,768]{1,0:T(8,128)(2,1)S(1)}, bf16[768,768]{1,0:T(8,128)(2,1)}, u32[]{:S(2)}) copy-start(bf16[768,768]{1,0:T(8,128)(2,1)} %copy-done.33) | copy-start | bytes 3538948
  622.7 150.6 %collective-permute-start.33 = (bf16[768,768]{1,0:T(8,128)(2,1)S(1)}, bf16[768,768]{1,0:T(8,128)(2,1)}, u32[]{:S(2)}, u32[]{:S(2)}) collective-permute-start(bf16[768,768]{1,0:T(8,128)(2,1)S(1)} %copy-done.50), channel_id=1, source_target_pairs={{0,16},{4,20},{8,24},{12,28},{16,0},{20,4},{24,8},{28,12},{1,17},{... | collective-permute-start | bytes 3538952 | tf_op jit(solution)/shard_map/ppermute | solution.py:34
  (38 other events, 1335.5 us)
Sparse Core Ops, SparseCore 0:
  39.9 65.4 all-gather.2

commit v2 on v1

--- a/solution.py
+++ b/solution.py
@@ -5,7 +5,8 @@
 from jax import lax
 from jax.sharding import PartitionSpec as P
 
-CHUNKS = 8
+CHUNKS = 24
+LAG = 4
 
 
 def slope_of(pre_value):
@@ -39,8 +40,8 @@
         x = lax.axis_index("dp") % 2
         if n_dp == 8 and n_mp == 4:
             rows = normed.shape[1] // 2
-            pieces = []
-            for flip in range(2):
+            pieces = [None, None]
+            for flip in (1, 0):
                 pairs = []
                 for d in range(n_dp):
                     hi, low, xs = d // 4, d // 2 % 2, d % 2
@@ -49,12 +50,12 @@
                         to_d = (hi * 2 + core) * 2 + (xs ^ flip)
                         pairs.append((d * n_mp + m, to_d * n_mp + y * 2 + low))
                 part = lax.dynamic_slice(normed, (0, (x ^ flip) * rows), (tokens, rows))
-                pieces.append(lax.ppermute(part, ("dp", "mp"), pairs))
-            full = lax.all_gather(jnp.stack(pieces), "mp", axis=0)
+                moved = lax.ppermute(part, ("dp", "mp"), pairs)
+                pieces[flip] = lax.all_gather(moved, "mp", axis=0)
             return [
                 [
                     [
-                        lax.dynamic_index_in_dim(full, hi * 2 + (lo ^ j), 0, keepdims=False)[k]
+                        lax.dynamic_index_in_dim(pieces[k], hi * 2 + (lo ^ j), 0, keepdims=False)
                         for hi in range(n_hi)
                     ]
                     for k in range(2)
@@ -80,26 +81,50 @@
         order = [(0, 0), (0, 1), (1, 0), (1, 1)]
         stacked = jnp.stack([jnp.concatenate([left[j][k][hi] for j, k in order]) for hi in range(n_hi)])
         width = pre_act.shape[1] // CHUNKS
-        out = jnp.zeros((stacked.shape[2], pre_act.shape[1]), jnp.bfloat16)
-        for i in range(CHUNKS):
+
+        def grad_chunk(i):
             cut = slice(i * width, (i + 1) * width)
             slope = slope_of(pre_act[:, cut].astype(jnp.float32))
-            own = (cotangent[:, cut].astype(jnp.float32) * slope).astype(jnp.bfloat16)
-            beside = move(own, 0, 1, 0)
-            across = move(own, 0, 0, 1)
-            both = move(beside, 0, 0, 1)
-            right = jnp.concatenate([own, across, beside, both])
+            return (cotangent[:, cut].astype(jnp.float32) * slope).astype(jnp.bfloat16)
 
-            def partial(step):
-                return contract_rows(
-                    lax.dynamic_index_in_dim(stacked, (my_hi + step) % n_hi, 0, keepdims=False), right
+        def partial(step, right):
+            block = lax.dynamic_index_in_dim(stacked, (my_hi + step) % n_hi, 0, keepdims=False)
+            return contract_rows(block, right)
+
+        out = jnp.zeros((stacked.shape[2], pre_act.shape[1]), jnp.bfloat16)
+        own, beside, across, both, right, sent = ({} for _ in range(6))
+        own[0], own[1] = grad_chunk(0), grad_chunk(1)
+        across[0] = move(own[0], 0, 0, 1)
+        for s in range(CHUNKS + LAG + 2):
+            hop, red, done = s - 1, s - LAG, s - LAG - 2
+            if s < CHUNKS:
+                beside[s] = move(own[s], 0, 1, 0)
+            if 0 <= hop < CHUNKS:
+                both[hop] = move(beside[hop], 0, 0, 1)
+            if s + 1 < CHUNKS:
+                across[s + 1] = move(own[s + 1], 0, 0, 1)
+            if 0 <= red < CHUNKS:
+                right[red] = jnp.concatenate([own[red], across[red], beside[red], both[red]])
+                sent[red] = [
+                    move(partial(step, right[red]).astype(jnp.bfloat16), step, 0, 0)
+                    for step in range(1, n_hi)
+                ]
+            if s + 2 < CHUNKS:
+                own[s + 2] = grad_chunk(s + 2)
+            ties = [
+                (table, i)
+                for table, i in (
+                    (beside, s), (both, hop), (across, s), (sent, red - 1), (own, s + 1), (own, s + 2)
                 )
-
-            sent = [move(partial(step).astype(jnp.bfloat16), step, 0, 0) for step in range(1, n_hi)]
-            total = partial(0)
-            for term in sent:
-                total = total + term.astype(jnp.float32)
-            out = lax.dynamic_update_slice(out, total.astype(jnp.bfloat16), (0, i * width))
+                if i in table
+            ]
+            for (table, i), value in zip(ties, lax.optimization_barrier([t[i] for t, i in ties])):
+                table[i] = value
+            if 0 <= done < CHUNKS:
+                total = partial(0, right[done])
+                for term in sent[done]:
+                    total = total + term.astype(jnp.float32)
+                out = lax.dynamic_update_slice(out, total.astype(jnp.bfloat16), (0, done * width))
         return out
 
     return local

time: 791 us -> 603 us (0.76)
  waiting for transfers between devices: 606 us -> 301 us
  starting transfers between devices: 46.7 us -> 114 us
  local copies, waits for them, and re-layouts: 9.22 us -> 38.3 us
  matrix products: 92.5 us -> 105 us
    ppermute x32 -> x96, waiting for transfers between devices: 533 us -> 274 us  [move(): return lax.ppermute(value, 'dp', dp_pairs(hi_step, lo_flip, x_flip))]
    ppermute x32 -> x96, starting transfers between devices: 43 us -> 110 us  [move(): return lax.ppermute(value, 'dp', dp_pairs(hi_step, lo_flip, x_flip))]
    all_gather x1 -> x2, waiting for transfers between devices: 47 us -> 0.02 us  [gather_left(): pieces[flip] = lax.all_gather(moved, 'mp', axis=0)]
    unnamed x102 -> x181, local copies, waits for them, and re-layouts: 0.65 us -> 14.1 us
    dot_general x16 -> x48, matrix products: 92.5 us -> 105 us  [contract_rows(): lax.dot_general(left, right, (((0,), (0,)), ((), ())), preferred_element_...]
    concatenate x0 -> x23, local copies, waits for them, and re-layouts: none -> 10.1 us  [local(): jnp.concatenate([own[red], across[red], beside[red], both[red]])]
    convert_element_type x1 -> x3, other arithmetic: 12.1 us -> 18.4 us  [grad_chunk(): return (cotangent[:, cut].astype(jnp.float32) * slope).astype(jnp.bfloat16)]
  transfers between devices with their start and end apart: 35 -> 100, of which waited for: 25 -> 34; matrix products, arithmetic and copies ran while one was open for 14% -> 27% of each run, Pallas kernels for 0% -> 0%
where the time goes in v2:
time: 603 us; the launch traced here: 596 us
  waiting for transfers between devices  301 us (50%)
  starting transfers between devices  114 us (19%)
  matrix products  105 us (17%)
  local copies, waits for them, and re-layouts  38.3 us (6%)
  other arithmetic  23 us (4%)
  between operations  15.2 us (3%)
    ppermute x96, waiting for transfers between devices, move(): return lax.ppermute(value, 'dp', dp_pairs(hi_step, lo_flip, x_flip))  274 us
    ppermute x96, starting transfers between devices, move(): return lax.ppermute(value, 'dp', dp_pairs(hi_step, lo_flip, x_flip))  110 us
    dot_general x48, matrix products, contract_rows(): lax.dot_general(left, right, (((0,), (0,)), ((), ())), preferred_element_...  105 us
    ppermute x2, waiting for transfers between devices, gather_left(): moved = lax.ppermute(part, ('dp', 'mp'), pairs)  26.8 us
    convert_element_type x3, other arithmetic, grad_chunk(): return (cotangent[:, cut].astype(jnp.float32) * slope).astype(jnp.bfloat16)  18.4 us
    unnamed x181, local copies, waits for them, and re-layouts  14.1 us
  transfers between devices with their start and end apart: 100, of which 34 were waited for; matrix products, arithmetic and copies ran while one was open for 27% of the time, Pallas kernels for 0%

profile of v2, /device:TPU:0, one launch (start us, length us, event | category | flops | bytes accessed | tf_op | source)
XLA Modules:
  0.0 596.3 jit_solution(12437427317745417392)
XLA Ops:
  8.3 3.0 collective-permute-start.1
  11.3 26.8 %collective-permute-done.1 = bf16[768,768]{1,0:T(8,128)(2,1)S(1)} collective-permute-done((bf16[768,768]{1,0:T(8,128)(2,1)S(1)}, bf16[768,768]{1,0:T(8,128)(2,1)S(1)}, u32[]{:S(2)}, u32[]{:S(2)}) %collective-permute-start.1) | collective-permute-done | bytes 1179680 | tf_op jit(solution)/shard_map/ppermute | solution.py:53
  41.1 4.4 fusion.236
  45.5 7.3 %collective-permute-start.2 = (bf16[768,256]{1,0:T(8,128)(2,1)S(1)}, bf16[768,256]{1,0:T(8,128)(2,1)S(1)}, u32[]{:S(2)}, u32[]{:S(2)}) collective-permute-start(bf16[768,256]{1,0:T(8,128)(2,1)S(1)} %get-tuple-element.302), channel_id=1, source_target_pairs={{0,8},{4,12},{8,0},{12,4},{16,24},{20,28},{24,16},{28,20},{1,9},{5... | collective-permute-start | bytes 1179656 | tf_op jit(solution)/shard_map/ppermute | solution.py:35
  54.9 7.0 %fusion.219 = (bf16[768,256]{1,0:T(8,128)(2,1)}, bf16[768,256]{1,0:T(8,128)(2,1)}, bf16[768,256]{1,0:T(8,128)(2,1)}, bf16[768,256]{1,0:T(8,128)(2,1)}, bf16[768,...) fusion(bf16[768,6144]{1,0:T(8,128)(2,1)} %param.4, ...), kind=kLoop, calls=%fused_computation.378 | loop fusion | flops 21233664 | bytes 10616832 | tf_op jit(solution)/shard_map/convert_element_type | solution.py:88
  66.5 7.0 %fusion.218 = (bf16[768,256]{1,0:T(8,128)(2,1)}, bf16[768,256]{1,0:T(8,128)(2,1)}, bf16[768,256]{1,0:T(8,128)(2,1)}, bf16[768,256]{1,0:T(8,128)(2,1)}, bf16[768,...) fusion(bf16[768,6144]{1,0:T(8,128)(2,1)} %param.4, ...), kind=kLoop, calls=%fused_computation.377 | loop fusion | flops 21233664 | bytes 10616832 | tf_op jit(solution)/shard_map/convert_element_type | solution.py:88
  74.0 7.8 %collective-permute-done.5 = bf16[768,256]{1,0:T(8,128)(2,1)S(1)} collective-permute-done((bf16[768,256]{1,0:T(8,128)(2,1)S(1)}, bf16[768,256]{1,0:T(8,128)(2,1)S(1)}, u32[]{:S(2)}, u32[]{:S(2)}) %collective-permute-start.5) | collective-permute-done | bytes 393248 | tf_op jit(solution)/shard_map/ppermute | solution.py:35
  84.8 5.4 collective-permute-done.9
  90.3 8.3 %collective-permute-done.8 = bf16[768,256]{1,0:T(8,128)(2,1)S(1)} collective-permute-done((bf16[768,256]{1,0:T(8,128)(2,1)S(1)}, bf16[768,256]{1,0:T(8,128)(2,1)S(1)}, u32[]{:S(2)}, u32[]{:S(2)}) %collective-permute-start.8) | collective-permute-done | bytes 393248 | tf_op jit(solution)/shard_map/ppermute | solution.py:35
  100.9 6.2 %collective-permute-done.12 = bf16[768,256]{1,0:T(8,128)(2,1)S(1)} collective-permute-done((bf16[768,256]{1,0:T(8,128)(2,1)S(1)}, bf16[768,256]{1,0:T(8,128)(2,1)S(1)}, u32[]{:S(2)}, u32[]{:S(2)}) %collective-permute-start.12) | collective-permute-done | bytes 393248 | tf_op jit(solution)/shard_map/ppermute | solution.py:35
  107.1 8.4 %collective-permute-done.11 = bf16[768,256]{1,0:T(8,128)(2,1)S(1)} collective-permute-done((bf16[768,256]{1,0:T(8,128)(2,1)S(1)}, bf16[768,256]{1,0:T(8,128)(2,1)S(1)}, u32[]{:S(2)}, u32[]{:S(2)}) %collective-permute-start.11) | collective-permute-done | bytes 393248 | tf_op jit(solution)/shard_map/ppermute | solution.py:35
  118.4 5.5 collective-permute-done.15
  123.9 8.4 %collective-permute-done.14 = bf16[768,256]{1,0:T(8,128)(2,1)S(1)} collective-permute-done((bf16[768,256]{1,0:T(8,128)(2,1)S(1)}, bf16[768,256]{1,0:T(8,128)(2,1)S(1)}, u32[]{:S(2)}, u32[]{:S(2)}) %collective-permute-start.14) | collective-permute-done | bytes 393248 | tf_op jit(solution)/shard_map/ppermute | solution.py:35
  137.0 4.6 dynamic-slice_bitcast_fusion.2
  146.0 3.9 fusion.3
  163.0 22.8 %collective-permute-done.19 = bf16[768,256]{1,0:T(8,128)(2,1)S(1)} collective-permute-done((bf16[768,256]{1,0:T(8,128)(2,1)S(1)}, bf16[768,256]{1,0:T(8,128)(2,1)S(1)}, u32[]{:S(2)}, u32[]{:S(2)}) %collective-permute-start.19) | collective-permute-done | bytes 393248 | tf_op jit(solution)/shard_map/ppermute | solution.py:35
  192.7 4.9 dynamic_update_slice.72
  199.4 2.9 convolution_convert_fusion.19
  202.3 3.4 collective-permute-start.31
  206.4 6.0 %collective-permute-done.20 = bf16[768,256]{1,0:T(8,128)(2,1)} collective-permute-done((bf16[768,256]{1,0:T(8,128)(2,1)}, bf16[768,256]{1,0:T(8,128)(2,1)}, u32[]{:S(2)}, u32[]{:S(2)}) %collective-permute-start.20) | collective-permute-done | bytes 393248 | tf_op jit(solution)/shard_map/ppermute | solution.py:35
  224.3 7.0 %collective-permute-done.24 = bf16[768,256]{1,0:T(8,128)(2,1)S(1)} collective-permute-done((bf16[768,256]{1,0:T(8,128)(2,1)S(1)}, bf16[768,256]{1,0:T(8,128)(2,1)S(1)}, u32[]{:S(2)}, u32[]{:S(2)}) %collective-permute-start.24) | collective-permute-done | bytes 393248 | tf_op jit(solution)/shard_map/ppermute | solution.py:35
  239.3 11.3 %collective-permute-done.28 = bf16[768,256]{1,0:T(8,128)(2,1)S(1)} collective-permute-done((bf16[768,256]{1,0:T(8,128)(2,1)S(1)}, bf16[768,256]{1,0:T(8,128)(2,1)S(1)}, u32[]{:S(2)}, u32[]{:S(2)}) %collective-permute-start.28) | collective-permute-done | bytes 393248 | tf_op jit(solution)/shard_map/ppermute | solution.py:35
  258.8 10.1 %collective-permute-done.32 = bf16[768,256]{1,0:T(8,128)(2,1)S(1)} collective-permute-done((bf16[768,256]{1,0:T(8,128)(2,1)S(1)}, bf16[768,256]{1,0:T(8,128)(2,1)S(1)}, u32[]{:S(2)}, u32[]{:S(2)}) %collective-permute-start.32) | collective-permute-done | bytes 393248 | tf_op jit(solution)/shard_map/ppermute | solution.py:35
  269.3 3.6 fusion.11
  274.4 4.1 collective-permute-start.47
  280.1 6.5 %collective-permute-done.36 = bf16[768,256]{1,0:T(8,128)(2,1)S(1)} collective-permute-done((bf16[768,256]{1,0:T(8,128)(2,1)S(1)}, bf16[768,256]{1,0:T(8,128)(2,1)S(1)}, u32[]{:S(2)}, u32[]{:S(2)}) %collective-permute-start.36) | collective-permute-done | bytes 393248 | tf_op jit(solution)/shard_map/ppermute | solution.py:35
  293.4 12.7 %collective-permute-done.40 = bf16[768,256]{1,0:T(8,128)(2,1)S(1)} collective-permute-done((bf16[768,256]{1,0:T(8,128)(2,1)S(1)}, bf16[768,256]{1,0:T(8,128)(2,1)S(1)}, u32[]{:S(2)}, u32[]{:S(2)}) %collective-permute-start.40) | collective-permute-done | bytes 393248 | tf_op jit(solution)/shard_map/ppermute | solution.py:35
  309.3 2.9 convolution_convert_fusion.13
  315.4 6.8 %collective-permute-done.44 = bf16[768,256]{1,0:T(8,128)(2,1)S(1)} collective-permute-done((bf16[768,256]{1,0:T(8,128)(2,1)S(1)}, bf16[768,256]{1,0:T(8,128)(2,1)S(1)}, u32[]{:S(2)}, u32[]{:S(2)}) %collective-permute-start.44) | collective-permute-done | bytes 393248 | tf_op jit(solution)/shard_map/ppermute | solution.py:35
  334.1 7.9 %collective-permute-done.48 = bf16[768,256]{1,0:T(8,128)(2,1)S(1)} collective-permute-done((bf16[768,256]{1,0:T(8,128)(2,1)S(1)}, bf16[768,256]{1,0:T(8,128)(2,1)S(1)}, u32[]{:S(2)}, u32[]{:S(2)}) %collective-permute-start.48) | collective-permute-done | bytes 393248 | tf_op jit(solution)/shard_map/ppermute | solution.py:35
  345.4 3.3 convolution_convert_fusion.11
  348.7 3.2 collective-permute-start.63
  352.4 7.2 %collective-permute-done.52 = bf16[768,256]{1,0:T(8,128)(2,1)S(1)} collective-permute-done((bf16[768,256]{1,0:T(8,128)(2,1)S(1)}, bf16[768,256]{1,0:T(8,128)(2,1)S(1)}, u32[]{:S(2)}, u32[]{:S(2)}) %collective-permute-start.52) | collective-permute-done | bytes 393248 | tf_op jit(solution)/shard_map/ppermute | solution.py:35
  367.0 2.9 collective-permute-start.67
  370.3 8.4 %collective-permute-done.56 = bf16[768,256]{1,0:T(8,128)(2,1)S(1)} collective-permute-done((bf16[768,256]{1,0:T(8,128)(2,1)S(1)}, bf16[768,256]{1,0:T(8,128)(2,1)S(1)}, u32[]{:S(2)}, u32[]{:S(2)}) %collective-permute-start.56) | collective-permute-done | bytes 393248 | tf_op jit(solution)/shard_map/ppermute | solution.py:35
  389.8 7.1 %collective-permute-done.60 = bf16[768,256]{1,0:T(8,128)(2,1)S(1)} collective-permute-done((bf16[768,256]{1,0:T(8,128)(2,1)S(1)}, bf16[768,256]{1,0:T(8,128)(2,1)S(1)}, u32[]{:S(2)}, u32[]{:S(2)}) %collective-permute-start.60) | collective-permute-done | bytes 393248 | tf_op jit(solution)/shard_map/ppermute | solution.py:35
  403.5 3.0 collective-permute-start.75
  407.5 8.8 %collective-permute-done.64 = bf16[768,256]{1,0:T(8,128)(2,1)S(1)} collective-permute-done((bf16[768,256]{1,0:T(8,128)(2,1)S(1)}, bf16[768,256]{1,0:T(8,128)(2,1)S(1)}, u32[]{:S(2)}, u32[]{:S(2)}) %collective-permute-start.64) | collective-permute-done | bytes 393248 | tf_op jit(solution)/shard_map/ppermute | solution.py:35
  427.0 6.5 %collective-permute-done.68 = bf16[768,256]{1,0:T(8,128)(2,1)S(1)} collective-permute-done((bf16[768,256]{1,0:T(8,128)(2,1)S(1)}, bf16[768,256]{1,0:T(8,128)(2,1)S(1)}, u32[]{:S(2)}, u32[]{:S(2)}) %collective-permute-start.68) | collective-permute-done | bytes 393248 | tf_op jit(solution)/shard_map/ppermute | solution.py:35
  444.5 8.5 %collective-permute-done.72 = bf16[768,256]{1,0:T(8,128)(2,1)S(1)} collective-permute-done((bf16[768,256]{1,0:T(8,128)(2,1)S(1)}, bf16[768,256]{1,0:T(8,128)(2,1)S(1)}, u32[]{:S(2)}, u32[]{:S(2)}) %collective-permute-start.72) | collective-permute-done | bytes 393248 | tf_op jit(solution)/shard_map/ppermute | solution.py:35
  463.8 6.9 %collective-permute-done.76 = bf16[768,256]{1,0:T(8,128)(2,1)S(1)} collective-permute-done((bf16[768,256]{1,0:T(8,128)(2,1)S(1)}, bf16[768,256]{1,0:T(8,128)(2,1)S(1)}, u32[]{:S(2)}, u32[]{:S(2)}) %collective-permute-start.76) | collective-permute-done | bytes 393248 | tf_op jit(solution)/shard_map/ppermute | solution.py:35
  479.4 11.0 %collective-permute-done.80 = bf16[768,256]{1,0:T(8,128)(2,1)S(1)} collective-permute-done((bf16[768,256]{1,0:T(8,128)(2,1)S(1)}, bf16[768,256]{1,0:T(8,128)(2,1)S(1)}, u32[]{:S(2)}, u32[]{:S(2)}) %collective-permute-start.80) | collective-permute-done | bytes 393248 | tf_op jit(solution)/shard_map/ppermute | solution.py:35
  498.9 10.0 %collective-permute-done.84 = bf16[768,256]{1,0:T(8,128)(2,1)S(1)} collective-permute-done((bf16[768,256]{1,0:T(8,128)(2,1)S(1)}, bf16[768,256]{1,0:T(8,128)(2,1)S(1)}, u32[]{:S(2)}, u32[]{:S(2)}) %collective-permute-start.84) | collective-permute-done | bytes 393248 | tf_op jit(solution)/shard_map/ppermute | solution.py:35
  513.9 18.5 %collective-permute-done.94 = bf16[768,256]{1,0:T(8,128)(2,1)S(1)} collective-permute-done((bf16[768,256]{1,0:T(8,128)(2,1)S(1)}, bf16[768,256]{1,0:T(8,128)(2,1)S(1)}, u32[]{:S(2)}, u32[]{:S(2)}) %collective-permute-start.94) | collective-permute-done | bytes 393248 | tf_op jit(solution)/shard_map/ppermute | solution.py:35
  535.0 7.3 %collective-permute-done.89 = bf16[768,256]{1,0:T(8,128)(2,1)S(1)} collective-permute-done((bf16[768,256]{1,0:T(8,128)(2,1)S(1)}, bf16[768,256]{1,0:T(8,128)(2,1)S(1)}, u32[]{:S(2)}, u32[]{:S(2)}) %collective-permute-start.89) | collective-permute-done | bytes 393248 | tf_op jit(solution)/shard_map/ppermute | solution.py:35
  545.0 16.7 %collective-permute-done.95 = bf16[768,256]{1,0:T(8,128)(2,1)S(1)} collective-permute-done((bf16[768,256]{1,0:T(8,128)(2,1)S(1)}, bf16[768,256]{1,0:T(8,128)(2,1)S(1)}, u32[]{:S(2)}, u32[]{:S(2)}) %collective-permute-start.95) | collective-permute-done | bytes 393248 | tf_op jit(solution)/shard_map/ppermute | solution.py:35
  572.2 6.3 %collective-permute-done.96 = bf16[768,256]{1,0:T(8,128)(2,1)S(1)} collective-permute-done((bf16[768,256]{1,0:T(8,128)(2,1)S(1)}, bf16[768,256]{1,0:T(8,128)(2,1)S(1)}, u32[]{:S(2)}, u32[]{:S(2)}) %collective-permute-start.96) | collective-permute-done | bytes 393248 | tf_op jit(solution)/shard_map/ppermute | solution.py:35
  580.7 6.1 %collective-permute-done.97 = bf16[768,256]{1,0:T(8,128)(2,1)S(1)} collective-permute-done((bf16[768,256]{1,0:T(8,128)(2,1)S(1)}, bf16[768,256]{1,0:T(8,128)(2,1)S(1)}, u32[]{:S(2)}, u32[]{:S(2)}) %collective-permute-start.97) | collective-permute-done | bytes 393248 | tf_op jit(solution)/shard_map/ppermute | solution.py:35
  (415 shorter events, 212.3 us)
Async XLA Ops:
  6.5 130.5 %all-gather.7.cloned.1.call-start = ((), (), s32[]{:S(2)}) async-start(), calls=%async_computation.1 | async-start | bytes 5898240 | tf_op jit(solution)/shard_map/all_gather | solution.py:54
  8.3 29.8 %collective-permute-start.1 = (bf16[768,768]{1,0:T(8,128)(2,1)S(1)}, bf16[768,768]{1,0:T(8,128)(2,1)S(1)}, u32[]{:S(2)}, u32[]{:S(2)}) collective-permute-start(bf16[768,768]{1,0:T(8,128)(2,1)S(1)} %get-tuple-element.314), channel_id=1, source_target_pairs={{0,4},{1,12},{2,6},{3,14},{4,0},{5,8},{6,2},{7,10},{8,5},{9,13},{1... | collective-permute-start | bytes 3538952 | tf_op jit(solution)/shard_map/ppermute | solution.py:53
  39.2 102.3 %all-gather.5.cloned.1.call-start = ((), (), s32[]{:S(2)}) async-start(), calls=%async_computation | async-start | bytes 5898240 | tf_op jit(solution)/shard_map/all_gather | solution.py:54
  54.4 19.6 %collective-permute-start.6 = (bf16[768,256]{1,0:T(8,128)(2,1)S(1)}, bf16[768,256]{1,0:T(8,128)(2,1)S(1)}, u32[]{:S(2)}, u32[]{:S(2)}) collective-permute-start(bf16[768,256]{1,0:T(8,128)(2,1)S(1)} %get-tuple-element.144), channel_id=1, source_target_pairs={{0,4},{4,0},{8,12},{12,8},{16,20},{20,16},{24,28},{28,24},{1,5},{5... | collective-permute-start | bytes 1179656 | tf_op jit(solution)/shard_map/ppermute | solution.py:35
  84.1 22.9 %collective-permute-start.12 = (bf16[768,256]{1,0:T(8,128)(2,1)S(1)}, bf16[768,256]{1,0:T(8,128)(2,1)S(1)}, u32[]{:S(2)}, u32[]{:S(2)}) collective-permute-start(bf16[768,256]{1,0:T(8,128)(2,1)S(1)} %get-tuple-element.150), channel_id=1, source_target_pairs={{0,4},{4,0},{8,12},{12,8},{16,20},{20,16},{24,28},{28,24},{1,5},{5... | collective-permute-start | bytes 1179656 | tf_op jit(solution)/shard_map/ppermute | solution.py:35
  100.2 23.7 %collective-permute-start.15 = (bf16[768,256]{1,0:T(8,128)(2,1)S(1)}, bf16[768,256]{1,0:T(8,128)(2,1)S(1)}, u32[]{:S(2)}, u32[]{:S(2)}) collective-permute-start(bf16[768,256]{1,0:T(8,128)(2,1)S(1)} %get-tuple-element.153), channel_id=1, source_target_pairs={{0,4},{4,0},{8,12},{12,8},{16,20},{20,16},{24,28},{28,24},{1,5},{5... | collective-permute-start | bytes 1179656 | tf_op jit(solution)/shard_map/ppermute | solution.py:35
  117.8 42.3 %collective-permute-start.18 = (bf16[768,256]{1,0:T(8,128)(2,1)S(1)}, bf16[768,256]{1,0:T(8,128)(2,1)}, u32[]{:S(2)}, u32[]{:S(2)}) collective-permute-start(bf16[768,256]{1,0:T(8,128)(2,1)S(1)} %get-tuple-element.156), channel_id=1, source_target_pairs={{0,4},{4,0},{8,12},{12,8},{16,20},{20,16},{24,28},{28,24},{1,5},{5... | collective-permute-start | bytes 1179656 | tf_op jit(solution)/shard_map/ppermute | solution.py:35
  132.3 27.9 %collective-permute-start.16 = (bf16[768,256]{1,0:T(8,128)(2,1)S(1)}, bf16[768,256]{1,0:T(8,128)(2,1)}, u32[]{:S(2)}, u32[]{:S(2)}) collective-permute-start(bf16[768,256]{1,0:T(8,128)(2,1)S(1)} %get-tuple-element.156), channel_id=1, source_target_pairs={{0,8},{4,12},{8,0},{12,4},{16,24},{20,28},{24,16},{28,20},{1,9},{5... | collective-permute-start | bytes 1179656 | tf_op jit(solution)/shard_map/ppermute | solution.py:35
  132.3 30.7 %collective-permute-start.17 = (bf16[768,256]{1,0:T(8,128)(2,1)}, bf16[768,256]{1,0:T(8,128)(2,1)}, u32[]{:S(2)}, u32[]{:S(2)}) collective-permute-start(bf16[768,256]{1,0:T(8,128)(2,1)} %collective-permute-done.13), channel_id=1, source_target_pairs={{0,4},{4,0},{8,12},{12,8},{16,20},{20,16},{24,28},{28,24},{1,5},{5... | collective-permute-start | bytes 1179656 | tf_op jit(solution)/shard_map/ppermute | solution.py:35
  133.9 68.4 %collective-permute-start.22 = (bf16[768,256]{1,0:T(8,128)(2,1)}, bf16[768,256]{1,0:T(8,128)(2,1)}, u32[]{:S(2)}, u32[]{:S(2)}) collective-permute-start(bf16[768,256]{1,0:T(8,128)(2,1)} %get-tuple-element.162), channel_id=1, source_target_pairs={{0,4},{4,0},{8,12},{12,8},{16,20},{20,16},{24,28},{28,24},{1,5},{5... | collective-permute-start | bytes 1179656 | tf_op jit(solution)/shard_map/ppermute | solution.py:35
  151.4 34.4 %collective-permute-start.19 = (bf16[768,256]{1,0:T(8,128)(2,1)S(1)}, bf16[768,256]{1,0:T(8,128)(2,1)S(1)}, u32[]{:S(2)}, u32[]{:S(2)}) collective-permute-start(bf16[768,256]{1,0:T(8,128)(2,1)S(1)} %convolution_convert_fusion.23), channel_id=1, source_target_pairs={{0,16},{4,20},{8,24},{12,28},{16,0},{20,4},{24,8},{28,12},{1,17},{... | collective-permute-start | bytes 1179656 | tf_op jit(solution)/shard_map/ppermute | solution.py:35
  160.1 45.6 %collective-permute-start.23 = (bf16[768,256]{1,0:T(8,128)(2,1)S(1)}, bf16[768,256]{1,0:T(8,128)(2,1)S(1)}, u32[]{:S(2)}, u32[]{:S(2)}) collective-permute-start(bf16[768,256]{1,0:T(8,128)(2,1)S(1)} %convolution_convert_fusion.22), channel_id=1, source_target_pairs={{0,16},{4,20},{8,24},{12,28},{16,0},{20,4},{24,8},{28,12},{1,17},{... | collective-permute-start | bytes 1179656 | tf_op jit(solution)/shard_map/ppermute | solution.py:35
  160.3 60.5 %collective-permute-start.27 = (bf16[768,256]{1,0:T(8,128)(2,1)}, bf16[768,256]{1,0:T(8,128)(2,1)S(1)}, u32[]{:S(2)}, u32[]{:S(2)}) collective-permute-start(bf16[768,256]{1,0:T(8,128)(2,1)} %convolution_convert_fusion.21), channel_id=1, source_target_pairs={{0,16},{4,20},{8,24},{12,28},{16,0},{20,4},{24,8},{28,12},{1,17},{... | collective-permute-start | bytes 1179656 | tf_op jit(solution)/shard_map/ppermute | solution.py:35
  185.9 26.5 %collective-permute-start.20 = (bf16[768,256]{1,0:T(8,128)(2,1)}, bf16[768,256]{1,0:T(8,128)(2,1)}, u32[]{:S(2)}, u32[]{:S(2)}) collective-permute-start(bf16[768,256]{1,0:T(8,128)(2,1)} %get-tuple-element.162), channel_id=1, source_target_pairs={{0,8},{4,12},{8,0},{12,4},{16,24},{20,28},{24,16},{28,20},{1,9},{5... | collective-permute-start | bytes 1179656 | tf_op jit(solution)/shard_map/ppermute | solution.py:35
  187.7 24.7 %collective-permute-start.21 = (bf16[768,256]{1,0:T(8,128)(2,1)}, bf16[768,256]{1,0:T(8,128)(2,1)}, u32[]{:S(2)}, u32[]{:S(2)}) collective-permute-start(bf16[768,256]{1,0:T(8,128)(2,1)} %collective-permute-done.16), channel_id=1, source_target_pairs={{0,4},{4,0},{8,12},{12,8},{16,20},{20,16},{24,28},{28,24},{1,5},{5... | collective-permute-start | bytes 1179656 | tf_op jit(solution)/shard_map/ppermute | solution.py:35
  202.3 33.6 %collective-permute-start.31 = (bf16[768,256]{1,0:T(8,128)(2,1)}, bf16[768,256]{1,0:T(8,128)(2,1)S(1)}, u32[]{:S(2)}, u32[]{:S(2)}) collective-permute-start(bf16[768,256]{1,0:T(8,128)(2,1)} %convolution_convert_fusion.20), channel_id=1, source_target_pairs={{0,16},{4,20},{8,24},{12,28},{16,0},{20,4},{24,8},{28,12},{1,17},{... | collective-permute-start | bytes 1179656 | tf_op jit(solution)/shard_map/ppermute | solution.py:35
  220.7 34.4 %collective-permute-start.35 = (bf16[768,256]{1,0:T(8,128)(2,1)S(1)}, bf16[768,256]{1,0:T(8,128)(2,1)S(1)}, u32[]{:S(2)}, u32[]{:S(2)}) collective-permute-start(bf16[768,256]{1,0:T(8,128)(2,1)S(1)} %convolution_convert_fusion.19), channel_id=1, source_target_pairs={{0,16},{4,20},{8,24},{12,28},{16,0},{20,4},{24,8},{28,12},{1,17},{... | collective-permute-start | bytes 1179656 | tf_op jit(solution)/shard_map/ppermute | solution.py:35
  235.9 38.5 %collective-permute-start.39 = (bf16[768,256]{1,0:T(8,128)(2,1)S(1)}, bf16[768,256]{1,0:T(8,128)(2,1)S(1)}, u32[]{:S(2)}, u32[]{:S(2)}) collective-permute-start(bf16[768,256]{1,0:T(8,128)(2,1)S(1)} %convolution_convert_fusion.18), channel_id=1, source_target_pairs={{0,16},{4,20},{8,24},{12,28},{16,0},{20,4},{24,8},{28,12},{1,17},{... | collective-permute-start | bytes 1179656 | tf_op jit(solution)/shard_map/ppermute | solution.py:35
  237.9 19.6 %collective-permute-start.34 = (bf16[768,256]{1,0:T(8,128)(2,1)S(1)}, bf16[768,256]{1,0:T(8,128)(2,1)S(1)}, u32[]{:S(2)}, u32[]{:S(2)}) collective-permute-start(bf16[768,256]{1,0:T(8,128)(2,1)S(1)} %copy-done.41), channel_id=1, source_target_pairs={{0,4},{4,0},{8,12},{12,8},{16,20},{20,16},{24,28},{28,24},{1,5},{5... | collective-permute-start | bytes 1179656 | tf_op jit(solution)/shard_map/ppermute | solution.py:35
  255.2 35.6 %collective-permute-start.43 = (bf16[768,256]{1,0:T(8,128)(2,1)S(1)}, bf16[768,256]{1,0:T(8,128)(2,1)S(1)}, u32[]{:S(2)}, u32[]{:S(2)}) collective-permute-start(bf16[768,256]{1,0:T(8,128)(2,1)S(1)} %convolution_convert_fusion.17), channel_id=1, source_target_pairs={{0,16},{4,20},{8,24},{12,28},{16,0},{20,4},{24,8},{28,12},{1,17},{... | collective-permute-start | bytes 1179656 | tf_op jit(solution)/shard_map/ppermute | solution.py:35
  257.5 20.9 %collective-permute-start.38 = (bf16[768,256]{1,0:T(8,128)(2,1)S(1)}, bf16[768,256]{1,0:T(8,128)(2,1)S(1)}, u32[]{:S(2)}, u32[]{:S(2)}) collective-permute-start(bf16[768,256]{1,0:T(8,128)(2,1)S(1)} %copy-done.40), channel_id=1, source_target_pairs={{0,4},{4,0},{8,12},{12,8},{16,20},{20,16},{24,28},{28,24},{1,5},{5... | collective-permute-start | bytes 1179656 | tf_op jit(solution)/shard_map/ppermute | solution.py:35
  274.4 37.8 %collective-permute-start.47 = (bf16[768,256]{1,0:T(8,128)(2,1)S(1)}, bf16[768,256]{1,0:T(8,128)(2,1)S(1)}, u32[]{:S(2)}, u32[]{:S(2)}) collective-permute-start(bf16[768,256]{1,0:T(8,128)(2,1)S(1)} %convolution_convert_fusion.16), channel_id=1, source_target_pairs={{0,16},{4,20},{8,24},{12,28},{16,0},{20,4},{24,8},{28,12},{1,17},{... | collective-permute-start | bytes 1179656 | tf_op jit(solution)/shard_map/ppermute | solution.py:35
  290.7 39.1 %collective-permute-start.51 = (bf16[768,256]{1,0:T(8,128)(2,1)S(1)}, bf16[768,256]{1,0:T(8,128)(2,1)S(1)}, u32[]{:S(2)}, u32[]{:S(2)}) collective-permute-start(bf16[768,256]{1,0:T(8,128)(2,1)S(1)} %convolution_convert_fusion.15), channel_id=1, source_target_pairs={{0,16},{4,20},{8,24},{12,28},{16,0},{20,4},{24,8},{28,12},{1,17},{... | collective-permute-start | bytes 1179656 | tf_op jit(solution)/shard_map/ppermute | solution.py:35
  292.4 21.5 %collective-permute-start.46 = (bf16[768,256]{1,0:T(8,128)(2,1)S(1)}, bf16[768,256]{1,0:T(8,128)(2,1)S(1)}, u32[]{:S(2)}, u32[]{:S(2)}) collective-permute-start(bf16[768,256]{1,0:T(8,128)(2,1)S(1)} %copy-done.38), channel_id=1, source_target_pairs={{0,4},{4,0},{8,12},{12,8},{16,20},{20,16},{24,28},{28,24},{1,5},{5... | collective-permute-start | bytes 1179656 | tf_op jit(solution)/shard_map/ppermute | solution.py:35
  312.2 36.6 %collective-permute-start.55 = (bf16[768,256]{1,0:T(8,128)(2,1)S(1)}, bf16[768,256]{1,0:T(8,128)(2,1)S(1)}, u32[]{:S(2)}, u32[]{:S(2)}) collective-permute-start(bf16[768,256]{1,0:T(8,128)(2,1)S(1)} %convolution_convert_fusion.14), channel_id=1, source_target_pairs={{0,16},{4,20},{8,24},{12,28},{16,0},{20,4},{24,8},{28,12},{1,17},{... | collective-permute-start | bytes 1179656 | tf_op jit(solution)/shard_map/ppermute | solution.py:35
  322.2 19.8 %collective-permute-start.48 = (bf16[768,256]{1,0:T(8,128)(2,1)S(1)}, bf16[768,256]{1,0:T(8,128)(2,1)S(1)}, u32[]{:S(2)}, u32[]{:S(2)}) collective-permute-start(bf16[768,256]{1,0:T(8,128)(2,1)S(1)} %copy-done.37), channel_id=1, source_target_pairs={{0,8},{4,12},{8,0},{12,4},{16,24},{20,28},{24,16},{28,20},{1,9},{5... | collective-permute-start | bytes 1179656 | tf_op jit(solution)/shard_map/ppermute | solution.py:35
  322.2 19.8 %collective-permute-start.49 = (bf16[768,256]{1,0:T(8,128)(2,1)S(1)}, bf16[768,256]{1,0:T(8,128)(2,1)S(1)}, u32[]{:S(2)}, u32[]{:S(2)}) collective-permute-start(bf16[768,256]{1,0:T(8,128)(2,1)S(1)} %collective-permute-done.44), channel_id=1, source_target_pairs={{0,4},{4,0},{8,12},{12,8},{16,20},{20,16},{24,28},{28,24},{1,5},{5... | collective-permute-start | bytes 1179656 | tf_op jit(solution)/shard_map/ppermute | solution.py:35
  329.9 37.1 %collective-permute-start.59 = (bf16[768,256]{1,0:T(8,128)(2,1)S(1)}, bf16[768,256]{1,0:T(8,128)(2,1)S(1)}, u32[]{:S(2)}, u32[]{:S(2)}) collective-permute-start(bf16[768,256]{1,0:T(8,128)(2,1)S(1)} %convolution_convert_fusion.13), channel_id=1, source_target_pairs={{0,16},{4,20},{8,24},{12,28},{16,0},{20,4},{24,8},{28,12},{1,17},{... | collective-permute-start | bytes 1179656 | tf_op jit(solution)/shard_map/ppermute | solution.py:35
  332.1 19.8 %collective-permute-start.54 = (bf16[768,256]{1,0:T(8,128)(2,1)S(1)}, bf16[768,256]{1,0:T(8,128)(2,1)S(1)}, u32[]{:S(2)}, u32[]{:S(2)}) collective-permute-start(bf16[768,256]{1,0:T(8,128)(2,1)S(1)} %copy-done.36), channel_id=1, source_target_pairs={{0,4},{4,0},{8,12},{12,8},{16,20},{20,16},{24,28},{28,24},{1,5},{5... | collective-permute-start | bytes 1179656 | tf_op jit(solution)/shard_map/ppermute | solution.py:35
  348.7 38.0 %collective-permute-start.63 = (bf16[768,256]{1,0:T(8,128)(2,1)S(1)}, bf16[768,256]{1,0:T(8,128)(2,1)S(1)}, u32[]{:S(2)}, u32[]{:S(2)}) collective-permute-start(bf16[768,256]{1,0:T(8,128)(2,1)S(1)} %convolution_convert_fusion.12), channel_id=1, source_target_pairs={{0,16},{4,20},{8,24},{12,28},{16,0},{20,4},{24,8},{28,12},{1,17},{... | collective-permute-start | bytes 1179656 | tf_op jit(solution)/shard_map/ppermute | solution.py:35
  367.0 36.5 %collective-permute-start.67 = (bf16[768,256]{1,0:T(8,128)(2,1)S(1)}, bf16[768,256]{1,0:T(8,128)(2,1)S(1)}, u32[]{:S(2)}, u32[]{:S(2)}) collective-permute-start(bf16[768,256]{1,0:T(8,128)(2,1)S(1)} %convolution_convert_fusion.11), channel_id=1, source_target_pairs={{0,16},{4,20},{8,24},{12,28},{16,0},{20,4},{24,8},{28,12},{1,17},{... | collective-permute-start | bytes 1179656 | tf_op jit(solution)/shard_map/ppermute | solution.py:35
  386.8 36.4 %collective-permute-start.71 = (bf16[768,256]{1,0:T(8,128)(2,1)S(1)}, bf16[768,256]{1,0:T(8,128)(2,1)S(1)}, u32[]{:S(2)}, u32[]{:S(2)}) collective-permute-start(bf16[768,256]{1,0:T(8,128)(2,1)S(1)} %convolution_convert_fusion.10), channel_id=1, source_target_pairs={{0,16},{4,20},{8,24},{12,28},{16,0},{20,4},{24,8},{28,12},{1,17},{... | collective-permute-start | bytes 1179656 | tf_op jit(solution)/shard_map/ppermute | solution.py:35
  396.8 19.5 %collective-permute-start.64 = (bf16[768,256]{1,0:T(8,128)(2,1)S(1)}, bf16[768,256]{1,0:T(8,128)(2,1)S(1)}, u32[]{:S(2)}, u32[]{:S(2)}) collective-permute-start(bf16[768,256]{1,0:T(8,128)(2,1)S(1)} %copy-done.33), channel_id=1, source_target_pairs={{0,8},{4,12},{8,0},{12,4},{16,24},{20,28},{24,16},{28,20},{1,9},{5... | collective-permute-start | bytes 1179656 | tf_op jit(solution)/shard_map/ppermute | solution.py:35
  403.5 37.4 %collective-permute-start.75 = (bf16[768,256]{1,0:T(8,128)(2,1)S(1)}, bf16[768,256]{1,0:T(8,128)(2,1)S(1)}, u32[]{:S(2)}, u32[]{:S(2)}) collective-permute-start(bf16[768,256]{1,0:T(8,128)(2,1)S(1)} %convolution_convert_fusion.9), channel_id=1, source_target_pairs={{0,16},{4,20},{8,24},{12,28},{16,0},{20,4},{24,8},{28,12},{1,17},{... | collective-permute-start | bytes 1179656 | tf_op jit(solution)/shard_map/ppermute | solution.py:35
  423.2 37.0 %collective-permute-start.79 = (bf16[768,256]{1,0:T(8,128)(2,1)S(1)}, bf16[768,256]{1,0:T(8,128)(2,1)S(1)}, u32[]{:S(2)}, u32[]{:S(2)}) collective-permute-start(bf16[768,256]{1,0:T(8,128)(2,1)S(1)} %convolution_convert_fusion.8), channel_id=1, source_target_pairs={{0,16},{4,20},{8,24},{12,28},{16,0},{20,4},{24,8},{28,12},{1,17},{... | collective-permute-start | bytes 1179656 | tf_op jit(solution)/shard_map/ppermute | solution.py:35
  440.9 34.7 %collective-permute-start.83 = (bf16[768,256]{1,0:T(8,128)(2,1)S(1)}, bf16[768,256]{1,0:T(8,128)(2,1)S(1)}, u32[]{:S(2)}, u32[]{:S(2)}) collective-permute-start(bf16[768,256]{1,0:T(8,128)(2,1)S(1)} %convolution_convert_fusion.7), channel_id=1, source_target_pairs={{0,16},{4,20},{8,24},{12,28},{16,0},{20,4},{24,8},{28,12},{1,17},{... | collective-permute-start | bytes 1179656 | tf_op jit(solution)/shard_map/ppermute | solution.py:35
  460.2 35.1 %collective-permute-start.87 = (bf16[768,256]{1,0:T(8,128)(2,1)S(1)}, bf16[768,256]{1,0:T(8,128)(2,1)S(1)}, u32[]{:S(2)}, u32[]{:S(2)}) collective-permute-start(bf16[768,256]{1,0:T(8,128)(2,1)S(1)} %convolution_convert_fusion.6), channel_id=1, source_target_pairs={{0,16},{4,20},{8,24},{12,28},{16,0},{20,4},{24,8},{28,12},{1,17},{... | collective-permute-start | bytes 1179656 | tf_op jit(solution)/shard_map/ppermute | solution.py:35
  470.8 19.7 %collective-permute-start.80 = (bf16[768,256]{1,0:T(8,128)(2,1)S(1)}, bf16[768,256]{1,0:T(8,128)(2,1)S(1)}, u32[]{:S(2)}, u32[]{:S(2)}) collective-permute-start(bf16[768,256]{1,0:T(8,128)(2,1)S(1)} %copy-done.29), channel_id=1, source_target_pairs={{0,8},{4,12},{8,0},{12,4},{16,24},{20,28},{24,16},{28,20},{1,9},{5... | collective-permute-start | bytes 1179656 | tf_op jit(solution)/shard_map/ppermute | solution.py:35
  470.8 19.6 %collective-permute-start.81 = (bf16[768,256]{1,0:T(8,128)(2,1)S(1)}, bf16[768,256]{1,0:T(8,128)(2,1)S(1)}, u32[]{:S(2)}, u32[]{:S(2)}) collective-permute-start(bf16[768,256]{1,0:T(8,128)(2,1)S(1)} %collective-permute-done.76), channel_id=1, source_target_pairs={{0,4},{4,0},{8,12},{12,8},{16,20},{20,16},{24,28},{28,24},{1,5},{5... | collective-permute-start | bytes 1179656 | tf_op jit(solution)/shard_map/ppermute | solution.py:35
  475.6 59.3 %collective-permute-start.91 = (bf16[768,256]{1,0:T(8,128)(2,1)S(1)}, bf16[768,256]{1,0:T(8,128)(2,1)S(1)}, u32[]{:S(2)}, u32[]{:S(2)}) collective-permute-start(bf16[768,256]{1,0:T(8,128)(2,1)S(1)} %convolution_convert_fusion.5), channel_id=1, source_target_pairs={{0,16},{4,20},{8,24},{12,28},{16,0},{20,4},{24,8},{28,12},{1,17},{... | collective-permute-start | bytes 1179656 | tf_op jit(solution)/shard_map/ppermute | solution.py:35
  495.3 68.5 %collective-permute-start.93 = (bf16[768,256]{1,0:T(8,128)(2,1)S(1)}, bf16[768,256]{1,0:T(8,128)(2,1)S(1)}, u32[]{:S(2)}, u32[]{:S(2)}) collective-permute-start(bf16[768,256]{1,0:T(8,128)(2,1)S(1)} %convolution_convert_fusion.4), channel_id=1, source_target_pairs={{0,16},{4,20},{8,24},{12,28},{16,0},{20,4},{24,8},{28,12},{1,17},{... | collective-permute-start | bytes 1179656 | tf_op jit(solution)/shard_map/ppermute | solution.py:35
  497.6 37.4 %collective-permute-start.90 = (bf16[768,256]{1,0:T(8,128)(2,1)S(1)}, bf16[768,256]{1,0:T(8,128)(2,1)S(1)}, u32[]{:S(2)}, u32[]{:S(2)}) collective-permute-start(bf16[768,256]{1,0:T(8,128)(2,1)S(1)} %copy-done.27), channel_id=1, source_target_pairs={{0,4},{4,0},{8,12},{12,8},{16,20},{20,16},{24,28},{28,24},{1,5},{5... | collective-permute-start | bytes 1179656 | tf_op jit(solution)/shard_map/ppermute | solution.py:35
  508.9 23.6 %collective-permute-start.94 = (bf16[768,256]{1,0:T(8,128)(2,1)S(1)}, bf16[768,256]{1,0:T(8,128)(2,1)S(1)}, u32[]{:S(2)}, u32[]{:S(2)}) collective-permute-start(bf16[768,256]{1,0:T(8,128)(2,1)S(1)} %convolution_convert_fusion.3), channel_id=1, source_target_pairs={{0,16},{4,20},{8,24},{12,28},{16,0},{20,4},{24,8},{28,12},{1,17},{... | collective-permute-start | bytes 1179656 | tf_op jit(solution)/shard_map/ppermute | solution.py:35
  509.1 25.9 %collective-permute-start.88 = (bf16[768,256]{1,0:T(8,128)(2,1)S(1)}, bf16[768,256]{1,0:T(8,128)(2,1)S(1)}, u32[]{:S(2)}, u32[]{:S(2)}) collective-permute-start(bf16[768,256]{1,0:T(8,128)(2,1)S(1)} %copy-done.27), channel_id=1, source_target_pairs={{0,8},{4,12},{8,0},{12,4},{16,24},{20,28},{24,16},{28,20},{1,9},{5... | collective-permute-start | bytes 1179656 | tf_op jit(solution)/shard_map/ppermute | solution.py:35
  534.9 26.8 %collective-permute-start.95 = (bf16[768,256]{1,0:T(8,128)(2,1)S(1)}, bf16[768,256]{1,0:T(8,128)(2,1)S(1)}, u32[]{:S(2)}, u32[]{:S(2)}) collective-permute-start(bf16[768,256]{1,0:T(8,128)(2,1)S(1)} %convolution_convert_fusion.2), channel_id=1, source_target_pairs={{0,16},{4,20},{8,24},{12,28},{16,0},{20,4},{24,8},{28,12},{1,17},{... | collective-permute-start | bytes 1179656 | tf_op jit(solution)/shard_map/ppermute | solution.py:35
  542.3 21.6 %collective-permute-start.92 = (bf16[768,256]{1,0:T(8,128)(2,1)S(1)}, bf16[768,256]{1,0:T(8,128)(2,1)S(1)}, u32[]{:S(2)}, u32[]{:S(2)}) collective-permute-start(bf16[768,256]{1,0:T(8,128)(2,1)S(1)} %collective-permute-done.88), channel_id=1, source_target_pairs={{0,4},{4,0},{8,12},{12,8},{16,20},{20,16},{24,28},{28,24},{1,5},{5... | collective-permute-start | bytes 1179656 | tf_op jit(solution)/shard_map/ppermute | solution.py:35
  544.8 33.7 %collective-permute-start.96 = (bf16[768,256]{1,0:T(8,128)(2,1)S(1)}, bf16[768,256]{1,0:T(8,128)(2,1)S(1)}, u32[]{:S(2)}, u32[]{:S(2)}) collective-permute-start(bf16[768,256]{1,0:T(8,128)(2,1)S(1)} %convolution_convert_fusion.1), channel_id=1, source_target_pairs={{0,16},{4,20},{8,24},{12,28},{16,0},{20,4},{24,8},{28,12},{1,17},{... | collective-permute-start | bytes 1179656 | tf_op jit(solution)/shard_map/ppermute | solution.py:35
  565.3 21.5 %collective-permute-start.97 = (bf16[768,256]{1,0:T(8,128)(2,1)S(1)}, bf16[768,256]{1,0:T(8,128)(2,1)S(1)}, u32[]{:S(2)}, u32[]{:S(2)}) collective-permute-start(bf16[768,256]{1,0:T(8,128)(2,1)S(1)} %convolution_convert_fusion), channel_id=1, source_target_pairs={{0,16},{4,20},{8,24},{12,28},{16,0},{20,4},{24,8},{28,12},{1,17},{... | collective-permute-start | bytes 1179656 | tf_op jit(solution)/shard_map/ppermute | solution.py:35
  (108 other events, 1252.9 us)
Sparse Core Ops, SparseCore 0:
  39.3 38.2 all-gather.6
  79.1 37.4 all-gather.4

commit v3 on v2

--- a/solution.py
+++ b/solution.py
@@ -6,7 +6,7 @@
 from jax.sharding import PartitionSpec as P
 
 CHUNKS = 24
-LAG = 4
+LAG = 2
 
 
 def slope_of(pre_value):

time: 603 us -> 567 us (0.940)
  waiting for transfers between devices: 301 us -> 250 us
  starting transfers between devices: 114 us -> 127 us
    ppermute x96, waiting for transfers between devices: 274 us -> 216 us  [move(): return lax.ppermute(value, 'dp', dp_pairs(hi_step, lo_flip, x_flip))]
    ppermute x96, starting transfers between devices: 110 us -> 124 us  [move(): return lax.ppermute(value, 'dp', dp_pairs(hi_step, lo_flip, x_flip))]
    all_gather x2, waiting for transfers between devices: 0.02 us -> 7.61 us  [gather_left(): pieces[flip] = lax.all_gather(moved, 'mp', axis=0)]
    unnamed x181 -> x169, local copies, waits for them, and re-layouts: 14.1 us -> 14.3 us
  transfers between devices with their start and end apart: 100 -> 100, of which waited for: 34 -> 34; matrix products, arithmetic and copies ran while one was open for 27% -> 28% of each run, Pallas kernels for 0% -> 0%
where the time goes in v3:
time: 567 us; the launch traced here: 558 us
  waiting for transfers between devices  250 us (44%)
  starting transfers between devices  127 us (22%)
  matrix products  104 us (18%)
  local copies, waits for them, and re-layouts  37.6 us (7%)
  other arithmetic  23.7 us (4%)
  between operations  15.2 us (3%)
    ppermute x96, waiting for transfers between devices, move(): return lax.ppermute(value, 'dp', dp_pairs(hi_step, lo_flip, x_flip))  216 us
    ppermute x96, starting transfers between devices, move(): return lax.ppermute(value, 'dp', dp_pairs(hi_step, lo_flip, x_flip))  124 us
    dot_general x48, matrix products, contract_rows(): lax.dot_general(left, right, (((0,), (0,)), ((), ())), preferred_element_...  104 us
    ppermute x2, waiting for transfers between devices, gather_left(): moved = lax.ppermute(part, ('dp', 'mp'), pairs)  26.8 us
    convert_element_type x3, other arithmetic, grad_chunk(): return (cotangent[:, cut].astype(jnp.float32) * slope).astype(jnp.bfloat16)  19.1 us
    unnamed x169, local copies, waits for them, and re-layouts  14.3 us
  transfers between devices with their start and end apart: 100, of which 34 were waited for; matrix products, arithmetic and copies ran while one was open for 28% of the time, Pallas kernels for 0%

profile of v3, /device:TPU:0, one launch (start us, length us, event | category | flops | bytes accessed | tf_op | source)
XLA Modules:
  0.0 558.1 jit_solution(146813112300762448)
XLA Ops:
  8.3 3.0 collective-permute-start.1
  11.3 26.8 %collective-permute-done.1 = bf16[768,768]{1,0:T(8,128)(2,1)S(1)} collective-permute-done((bf16[768,768]{1,0:T(8,128)(2,1)S(1)}, bf16[768,768]{1,0:T(8,128)(2,1)S(1)}, u32[]{:S(2)}, u32[]{:S(2)}) %collective-permute-start.1) | collective-permute-done | bytes 1179680 | tf_op jit(solution)/shard_map/ppermute | solution.py:53
  41.0 5.2 fusion.236
  46.3 7.5 %collective-permute-start.2 = (bf16[768,256]{1,0:T(8,128)(2,1)S(1)}, bf16[768,256]{1,0:T(8,128)(2,1)S(1)}, u32[]{:S(2)}, u32[]{:S(2)}) collective-permute-start(bf16[768,256]{1,0:T(8,128)(2,1)S(1)} %get-tuple-element.306), channel_id=1, source_target_pairs={{0,8},{4,12},{8,0},{12,4},{16,24},{20,28},{24,16},{28,20},{1,9},{5... | collective-permute-start | bytes 1179656 | tf_op jit(solution)/shard_map/ppermute | solution.py:35
  55.8 6.9 %fusion.219 = (bf16[768,256]{1,0:T(8,128)(2,1)}, bf16[768,256]{1,0:T(8,128)(2,1)}, bf16[768,256]{1,0:T(8,128)(2,1)}, bf16[768,256]{1,0:T(8,128)(2,1)}, bf16[768,...) fusion(bf16[768,6144]{1,0:T(8,128)(2,1)} %param.4, ...), kind=kLoop, calls=%fused_computation.378 | loop fusion | flops 21233664 | bytes 10616832 | tf_op jit(solution)/shard_map/convert_element_type | solution.py:88
  67.3 7.0 %fusion.218 = (bf16[768,256]{1,0:T(8,128)(2,1)}, bf16[768,256]{1,0:T(8,128)(2,1)}, bf16[768,256]{1,0:T(8,128)(2,1)}, bf16[768,256]{1,0:T(8,128)(2,1)}, bf16[768,...) fusion(bf16[768,6144]{1,0:T(8,128)(2,1)} %param.4, ...), kind=kLoop, calls=%fused_computation.377 | loop fusion | flops 21233664 | bytes 10616832 | tf_op jit(solution)/shard_map/convert_element_type | solution.py:88
  74.8 7.8 %collective-permute-done.5 = bf16[768,256]{1,0:T(8,128)(2,1)S(1)} collective-permute-done((bf16[768,256]{1,0:T(8,128)(2,1)S(1)}, bf16[768,256]{1,0:T(8,128)(2,1)S(1)}, u32[]{:S(2)}, u32[]{:S(2)}) %collective-permute-start.5) | collective-permute-done | bytes 393248 | tf_op jit(solution)/shard_map/ppermute | solution.py:35
  87.0 4.0 collective-permute-done.9
  91.1 8.4 %collective-permute-done.8 = bf16[768,256]{1,0:T(8,128)(2,1)S(1)} collective-permute-done((bf16[768,256]{1,0:T(8,128)(2,1)S(1)}, bf16[768,256]{1,0:T(8,128)(2,1)S(1)}, u32[]{:S(2)}, u32[]{:S(2)}) %collective-permute-start.8) | collective-permute-done | bytes 393248 | tf_op jit(solution)/shard_map/ppermute | solution.py:35
  104.4 4.6 dynamic-slice_bitcast_fusion.2
  109.0 7.6 %all-gather.5.cloned.1.call-done = bf16[3072,768]{1,0:T(8,128)(2,1)} async-done(((bf16[768,768]{1,0:T(8,128)(2,1)}), bf16[3072,768]{1,0:T(8,128)(2,1)}) %all-gather.5.cloned.1.call-update) | async-done | bytes 4718608 | tf_op jit(solution)/shard_map/all_gather | solution.py:54
  121.1 3.9 fusion.3
  132.4 23.8 %collective-permute-done.13 = bf16[768,256]{1,0:T(8,128)(2,1)S(1)} collective-permute-done((bf16[768,256]{1,0:T(8,128)(2,1)S(1)}, bf16[768,256]{1,0:T(8,128)(2,1)S(1)}, u32[]{:S(2)}, u32[]{:S(2)}) %collective-permute-start.13) | collective-permute-done | bytes 393248 | tf_op jit(solution)/shard_map/ppermute | solution.py:35
  162.9 4.9 dynamic_update_slice.72
  170.3 3.3 collective-permute-start.21
  176.9 3.6 fusion.5
  184.6 8.7 %collective-permute-done.21 = bf16[768,256]{1,0:T(8,128)(2,1)S(1)} collective-permute-done((bf16[768,256]{1,0:T(8,128)(2,1)S(1)}, bf16[768,256]{1,0:T(8,128)(2,1)S(1)}, u32[]{:S(2)}, u32[]{:S(2)}) %collective-permute-start.21) | collective-permute-done | bytes 393248 | tf_op jit(solution)/shard_map/ppermute | solution.py:35
  201.1 7.4 %collective-permute-start.29 = (bf16[768,256]{1,0:T(8,128)(2,1)S(1)}, bf16[768,256]{1,0:T(8,128)(2,1)S(1)}, u32[]{:S(2)}, u32[]{:S(2)}) collective-permute-start(bf16[768,256]{1,0:T(8,128)(2,1)S(1)} %convolution_convert_fusion.19), channel_id=1, source_target_pairs={{0,16},{4,20},{8,24},{12,28},{16,0},{20,4},{24,8},{28,12},{1,17},{... | collective-permute-start | bytes 1179656 | tf_op jit(solution)/shard_map/ppermute | solution.py:35
  218.4 7.7 %collective-permute-start.33 = (bf16[768,256]{1,0:T(8,128)(2,1)S(1)}, bf16[768,256]{1,0:T(8,128)(2,1)S(1)}, u32[]{:S(2)}, u32[]{:S(2)}) collective-permute-start(bf16[768,256]{1,0:T(8,128)(2,1)S(1)} %convolution_convert_fusion.18), channel_id=1, source_target_pairs={{0,16},{4,20},{8,24},{12,28},{16,0},{20,4},{24,8},{28,12},{1,17},{... | collective-permute-start | bytes 1179656 | tf_op jit(solution)/shard_map/ppermute | solution.py:35
  226.3 7.2 %collective-permute-done.26 = bf16[768,256]{1,0:T(8,128)(2,1)S(1)} collective-permute-done((bf16[768,256]{1,0:T(8,128)(2,1)S(1)}, bf16[768,256]{1,0:T(8,128)(2,1)S(1)}, u32[]{:S(2)}, u32[]{:S(2)}) %collective-permute-start.26) | collective-permute-done | bytes 393248 | tf_op jit(solution)/shard_map/ppermute | solution.py:35
  239.4 3.5 collective-permute-start.37
  242.9 8.2 %collective-permute-done.30 = bf16[768,256]{1,0:T(8,128)(2,1)S(1)} collective-permute-done((bf16[768,256]{1,0:T(8,128)(2,1)S(1)}, bf16[768,256]{1,0:T(8,128)(2,1)S(1)}, u32[]{:S(2)}, u32[]{:S(2)}) %collective-permute-start.30) | collective-permute-done | bytes 393248 | tf_op jit(solution)/shard_map/ppermute | solution.py:35
  258.9 9.9 %collective-permute-done.34 = bf16[768,256]{1,0:T(8,128)(2,1)S(1)} collective-permute-done((bf16[768,256]{1,0:T(8,128)(2,1)S(1)}, bf16[768,256]{1,0:T(8,128)(2,1)S(1)}, u32[]{:S(2)}, u32[]{:S(2)}) %collective-permute-start.34) | collective-permute-done | bytes 393248 | tf_op jit(solution)/shard_map/ppermute | solution.py:35
  275.6 11.0 %collective-permute-done.38 = bf16[768,256]{1,0:T(8,128)(2,1)S(1)} collective-permute-done((bf16[768,256]{1,0:T(8,128)(2,1)S(1)}, bf16[768,256]{1,0:T(8,128)(2,1)S(1)}, u32[]{:S(2)}, u32[]{:S(2)}) %collective-permute-start.38) | collective-permute-done | bytes 393248 | tf_op jit(solution)/shard_map/ppermute | solution.py:35
  292.6 10.8 %collective-permute-done.42 = bf16[768,256]{1,0:T(8,128)(2,1)S(1)} collective-permute-done((bf16[768,256]{1,0:T(8,128)(2,1)S(1)}, bf16[768,256]{1,0:T(8,128)(2,1)S(1)}, u32[]{:S(2)}, u32[]{:S(2)}) %collective-permute-start.42) | collective-permute-done | bytes 393248 | tf_op jit(solution)/shard_map/ppermute | solution.py:35
  312.4 6.8 %collective-permute-done.46 = bf16[768,256]{1,0:T(8,128)(2,1)S(1)} collective-permute-done((bf16[768,256]{1,0:T(8,128)(2,1)S(1)}, bf16[768,256]{1,0:T(8,128)(2,1)S(1)}, u32[]{:S(2)}, u32[]{:S(2)}) %collective-permute-start.46) | collective-permute-done | bytes 393248 | tf_op jit(solution)/shard_map/ppermute | solution.py:35
  324.3 3.4 convolution_convert_fusion.12
  328.4 4.8 collective-permute-done.53
  344.5 6.0 %collective-permute-done.57 = bf16[768,256]{1,0:T(8,128)(2,1)S(1)} collective-permute-done((bf16[768,256]{1,0:T(8,128)(2,1)S(1)}, bf16[768,256]{1,0:T(8,128)(2,1)S(1)}, u32[]{:S(2)}, u32[]{:S(2)}) %collective-permute-start.57) | collective-permute-done | bytes 393248 | tf_op jit(solution)/shard_map/ppermute | solution.py:35
  358.8 3.3 collective-permute-start.65
  362.1 6.8 %collective-permute-done.61 = bf16[768,256]{1,0:T(8,128)(2,1)S(1)} collective-permute-done((bf16[768,256]{1,0:T(8,128)(2,1)S(1)}, bf16[768,256]{1,0:T(8,128)(2,1)S(1)}, u32[]{:S(2)}, u32[]{:S(2)}) %collective-permute-start.61) | collective-permute-done | bytes 393248 | tf_op jit(solution)/shard_map/ppermute | solution.py:35
  374.2 3.0 convolution_convert_fusion.9
  380.2 6.9 %collective-permute-done.62 = bf16[768,256]{1,0:T(8,128)(2,1)S(1)} collective-permute-done((bf16[768,256]{1,0:T(8,128)(2,1)S(1)}, bf16[768,256]{1,0:T(8,128)(2,1)S(1)}, u32[]{:S(2)}, u32[]{:S(2)}) %collective-permute-start.62) | collective-permute-done | bytes 393248 | tf_op jit(solution)/shard_map/ppermute | solution.py:35
  396.6 10.0 %collective-permute-done.66 = bf16[768,256]{1,0:T(8,128)(2,1)S(1)} collective-permute-done((bf16[768,256]{1,0:T(8,128)(2,1)S(1)}, bf16[768,256]{1,0:T(8,128)(2,1)S(1)}, u32[]{:S(2)}, u32[]{:S(2)}) %collective-permute-start.66) | collective-permute-done | bytes 393248 | tf_op jit(solution)/shard_map/ppermute | solution.py:35
  411.8 3.0 convolution_convert_fusion.7
  414.9 10.0 %collective-permute-done.70 = bf16[768,256]{1,0:T(8,128)(2,1)S(1)} collective-permute-done((bf16[768,256]{1,0:T(8,128)(2,1)S(1)}, bf16[768,256]{1,0:T(8,128)(2,1)S(1)}, u32[]{:S(2)}, u32[]{:S(2)}) %collective-permute-start.70) | collective-permute-done | bytes 393248 | tf_op jit(solution)/shard_map/ppermute | solution.py:35
  430.0 3.0 convolution_convert_fusion.6
  434.6 8.3 %collective-permute-done.74 = bf16[768,256]{1,0:T(8,128)(2,1)S(1)} collective-permute-done((bf16[768,256]{1,0:T(8,128)(2,1)S(1)}, bf16[768,256]{1,0:T(8,128)(2,1)S(1)}, u32[]{:S(2)}, u32[]{:S(2)}) %collective-permute-start.74) | collective-permute-done | bytes 393248 | tf_op jit(solution)/shard_map/ppermute | solution.py:35
  448.1 3.1 convolution_convert_fusion.5
  453.7 4.9 collective-permute-done.78
  464.9 5.9 %collective-permute-start.89 = (bf16[768,256]{1,0:T(8,128)(2,1)S(1)}, bf16[768,256]{1,0:T(8,128)(2,1)S(1)}, u32[]{:S(2)}, u32[]{:S(2)}) collective-permute-start(bf16[768,256]{1,0:T(8,128)(2,1)S(1)} %convolution_convert_fusion.4), channel_id=1, source_target_pairs={{0,16},{4,20},{8,24},{12,28},{16,0},{20,4},{24,8},{28,12},{1,17},{... | collective-permute-start | bytes 1179656 | tf_op jit(solution)/shard_map/ppermute | solution.py:35
  470.8 5.4 collective-permute-done.82
  482.4 8.5 %collective-permute-start.93 = (bf16[768,256]{1,0:T(8,128)(2,1)S(1)}, bf16[768,256]{1,0:T(8,128)(2,1)S(1)}, u32[]{:S(2)}, u32[]{:S(2)}) collective-permute-start(bf16[768,256]{1,0:T(8,128)(2,1)S(1)} %convolution_convert_fusion.3), channel_id=1, source_target_pairs={{0,16},{4,20},{8,24},{12,28},{16,0},{20,4},{24,8},{28,12},{1,17},{... | collective-permute-start | bytes 1179656 | tf_op jit(solution)/shard_map/ppermute | solution.py:35
  490.8 3.8 collective-permute-done.86
  498.2 6.6 %collective-permute-start.95 = (bf16[768,256]{1,0:T(8,128)(2,1)S(1)}, bf16[768,256]{1,0:T(8,128)(2,1)S(1)}, u32[]{:S(2)}, u32[]{:S(2)}) collective-permute-start(bf16[768,256]{1,0:T(8,128)(2,1)S(1)} %convolution_convert_fusion.2), channel_id=1, source_target_pairs={{0,16},{4,20},{8,24},{12,28},{16,0},{20,4},{24,8},{28,12},{1,17},{... | collective-permute-start | bytes 1179656 | tf_op jit(solution)/shard_map/ppermute | solution.py:35
  507.1 14.4 %collective-permute-done.93 = bf16[768,256]{1,0:T(8,128)(2,1)S(1)} collective-permute-done((bf16[768,256]{1,0:T(8,128)(2,1)S(1)}, bf16[768,256]{1,0:T(8,128)(2,1)S(1)}, u32[]{:S(2)}, u32[]{:S(2)}) %collective-permute-start.93) | collective-permute-done | bytes 393248 | tf_op jit(solution)/shard_map/ppermute | solution.py:35
  525.7 8.5 %collective-permute-done.95 = bf16[768,256]{1,0:T(8,128)(2,1)S(1)} collective-permute-done((bf16[768,256]{1,0:T(8,128)(2,1)S(1)}, bf16[768,256]{1,0:T(8,128)(2,1)S(1)}, u32[]{:S(2)}, u32[]{:S(2)}) %collective-permute-start.95) | collective-permute-done | bytes 393248 | tf_op jit(solution)/shard_map/ppermute | solution.py:35
  537.9 6.5 %collective-permute-done.96 = bf16[768,256]{1,0:T(8,128)(2,1)S(1)} collective-permute-done((bf16[768,256]{1,0:T(8,128)(2,1)S(1)}, bf16[768,256]{1,0:T(8,128)(2,1)S(1)}, u32[]{:S(2)}, u32[]{:S(2)}) %collective-permute-start.96) | collective-permute-done | bytes 393248 | tf_op jit(solution)/shard_map/ppermute | solution.py:35
  (403 shorter events, 197.3 us)
Async XLA Ops:
  6.5 97.9 %all-gather.7.cloned.1.call-start = ((), (), s32[]{:S(2)}) async-start(), calls=%async_computation.1 | async-start | bytes 5898240 | tf_op jit(solution)/shard_map/all_gather | solution.py:54
  8.3 29.8 %collective-permute-start.1 = (bf16[768,768]{1,0:T(8,128)(2,1)S(1)}, bf16[768,768]{1,0:T(8,128)(2,1)S(1)}, u32[]{:S(2)}, u32[]{:S(2)}) collective-permute-start(bf16[768,768]{1,0:T(8,128)(2,1)S(1)} %get-tuple-element.318), channel_id=1, source_target_pairs={{0,4},{1,12},{2,6},{3,14},{4,0},{5,8},{6,2},{7,10},{8,5},{9,13},{1... | collective-permute-start | bytes 3538952 | tf_op jit(solution)/shard_map/ppermute | solution.py:53
  39.2 77.4 %all-gather.5.cloned.1.call-start = ((), (), s32[]{:S(2)}) async-start(), calls=%async_computation | async-start | bytes 5898240 | tf_op jit(solution)/shard_map/all_gather | solution.py:54
  84.9 46.9 %collective-permute-start.12 = (bf16[768,256]{1,0:T(8,128)(2,1)}, bf16[768,256]{1,0:T(8,128)(2,1)}, u32[]{:S(2)}, u32[]{:S(2)}) collective-permute-start(bf16[768,256]{1,0:T(8,128)(2,1)} %get-tuple-element.152), channel_id=1, source_target_pairs={{0,4},{4,0},{8,12},{12,8},{16,20},{20,16},{24,28},{28,24},{1,5},{5... | collective-permute-start | bytes 1179656 | tf_op jit(solution)/shard_map/ppermute | solution.py:35
  99.5 32.9 %collective-permute-start.10 = (bf16[768,256]{1,0:T(8,128)(2,1)}, bf16[768,256]{1,0:T(8,128)(2,1)}, u32[]{:S(2)}, u32[]{:S(2)}) collective-permute-start(bf16[768,256]{1,0:T(8,128)(2,1)} %get-tuple-element.152), channel_id=1, source_target_pairs={{0,8},{4,12},{8,0},{12,4},{16,24},{20,28},{24,16},{28,20},{1,9},{5... | collective-permute-start | bytes 1179656 | tf_op jit(solution)/shard_map/ppermute | solution.py:35
  99.5 32.9 %collective-permute-start.11 = (bf16[768,256]{1,0:T(8,128)(2,1)}, bf16[768,256]{1,0:T(8,128)(2,1)}, u32[]{:S(2)}, u32[]{:S(2)}) collective-permute-start(bf16[768,256]{1,0:T(8,128)(2,1)} %collective-permute-done.7), channel_id=1, source_target_pairs={{0,4},{4,0},{8,12},{12,8},{16,20},{20,16},{24,28},{28,24},{1,5},{5... | collective-permute-start | bytes 1179656 | tf_op jit(solution)/shard_map/ppermute | solution.py:35
  101.0 69.2 %collective-permute-start.16 = (bf16[768,256]{1,0:T(8,128)(2,1)}, bf16[768,256]{1,0:T(8,128)(2,1)}, u32[]{:S(2)}, u32[]{:S(2)}) collective-permute-start(bf16[768,256]{1,0:T(8,128)(2,1)} %get-tuple-element.158), channel_id=1, source_target_pairs={{0,4},{4,0},{8,12},{12,8},{16,20},{20,16},{24,28},{28,24},{1,5},{5... | collective-permute-start | bytes 1179656 | tf_op jit(solution)/shard_map/ppermute | solution.py:35
  126.5 29.8 %collective-permute-start.13 = (bf16[768,256]{1,0:T(8,128)(2,1)S(1)}, bf16[768,256]{1,0:T(8,128)(2,1)S(1)}, u32[]{:S(2)}, u32[]{:S(2)}) collective-permute-start(bf16[768,256]{1,0:T(8,128)(2,1)S(1)} %convolution_convert_fusion.23), channel_id=1, source_target_pairs={{0,16},{4,20},{8,24},{12,28},{16,0},{20,4},{24,8},{28,12},{1,17},{... | collective-permute-start | bytes 1179656 | tf_op jit(solution)/shard_map/ppermute | solution.py:35
  131.8 41.8 %collective-permute-start.17 = (bf16[768,256]{1,0:T(8,128)(2,1)S(1)}, bf16[768,256]{1,0:T(8,128)(2,1)S(1)}, u32[]{:S(2)}, u32[]{:S(2)}) collective-permute-start(bf16[768,256]{1,0:T(8,128)(2,1)S(1)} %convolution_convert_fusion.22), channel_id=1, source_target_pairs={{0,16},{4,20},{8,24},{12,28},{16,0},{20,4},{24,8},{28,12},{1,17},{... | collective-permute-start | bytes 1179656 | tf_op jit(solution)/shard_map/ppermute | solution.py:35
  158.8 23.1 %collective-permute-start.20 = (bf16[768,256]{1,0:T(8,128)(2,1)S(1)}, bf16[768,256]{1,0:T(8,128)(2,1)}, u32[]{:S(2)}, u32[]{:S(2)}) collective-permute-start(bf16[768,256]{1,0:T(8,128)(2,1)S(1)} %get-tuple-element.164), channel_id=1, source_target_pairs={{0,4},{4,0},{8,12},{12,8},{16,20},{20,16},{24,28},{28,24},{1,5},{5... | collective-permute-start | bytes 1179656 | tf_op jit(solution)/shard_map/ppermute | solution.py:35
  170.3 23.0 %collective-permute-start.21 = (bf16[768,256]{1,0:T(8,128)(2,1)S(1)}, bf16[768,256]{1,0:T(8,128)(2,1)S(1)}, u32[]{:S(2)}, u32[]{:S(2)}) collective-permute-start(bf16[768,256]{1,0:T(8,128)(2,1)S(1)} %convolution_convert_fusion.21), channel_id=1, source_target_pairs={{0,16},{4,20},{8,24},{12,28},{16,0},{20,4},{24,8},{28,12},{1,17},{... | collective-permute-start | bytes 1179656 | tf_op jit(solution)/shard_map/ppermute | solution.py:35
  173.6 19.7 %collective-permute-start.18 = (bf16[768,256]{1,0:T(8,128)(2,1)S(1)}, bf16[768,256]{1,0:T(8,128)(2,1)S(1)}, u32[]{:S(2)}, u32[]{:S(2)}) collective-permute-start(bf16[768,256]{1,0:T(8,128)(2,1)S(1)} %get-tuple-element.164), channel_id=1, source_target_pairs={{0,8},{4,12},{8,0},{12,4},{16,24},{20,28},{24,16},{28,20},{1,9},{5... | collective-permute-start | bytes 1179656 | tf_op jit(solution)/shard_map/ppermute | solution.py:35
  175.3 25.9 %collective-permute-start.24 = (bf16[768,256]{1,0:T(8,128)(2,1)S(1)}, bf16[768,256]{1,0:T(8,128)(2,1)S(1)}, u32[]{:S(2)}, u32[]{:S(2)}) collective-permute-start(bf16[768,256]{1,0:T(8,128)(2,1)S(1)} %copy-done.39), channel_id=1, source_target_pairs={{0,4},{4,0},{8,12},{12,8},{16,20},{20,16},{24,28},{28,24},{1,5},{5... | collective-permute-start | bytes 1179656 | tf_op jit(solution)/shard_map/ppermute | solution.py:35
  182.0 27.9 %collective-permute-start.25 = (bf16[768,256]{1,0:T(8,128)(2,1)S(1)}, bf16[768,256]{1,0:T(8,128)(2,1)S(1)}, u32[]{:S(2)}, u32[]{:S(2)}) collective-permute-start(bf16[768,256]{1,0:T(8,128)(2,1)S(1)} %convolution_convert_fusion.20), channel_id=1, source_target_pairs={{0,16},{4,20},{8,24},{12,28},{16,0},{20,4},{24,8},{28,12},{1,17},{... | collective-permute-start | bytes 1179656 | tf_op jit(solution)/shard_map/ppermute | solution.py:35
  195.7 22.8 %collective-permute-start.28 = (bf16[768,256]{1,0:T(8,128)(2,1)S(1)}, bf16[768,256]{1,0:T(8,128)(2,1)S(1)}, u32[]{:S(2)}, u32[]{:S(2)}) collective-permute-start(bf16[768,256]{1,0:T(8,128)(2,1)S(1)} %copy-done.38), channel_id=1, source_target_pairs={{0,4},{4,0},{8,12},{12,8},{16,20},{20,16},{24,28},{28,24},{1,5},{5... | collective-permute-start | bytes 1179656 | tf_op jit(solution)/shard_map/ppermute | solution.py:35
  201.1 25.2 %collective-permute-start.29 = (bf16[768,256]{1,0:T(8,128)(2,1)S(1)}, bf16[768,256]{1,0:T(8,128)(2,1)S(1)}, u32[]{:S(2)}, u32[]{:S(2)}) collective-permute-start(bf16[768,256]{1,0:T(8,128)(2,1)S(1)} %convolution_convert_fusion.19), channel_id=1, source_target_pairs={{0,16},{4,20},{8,24},{12,28},{16,0},{20,4},{24,8},{28,12},{1,17},{... | collective-permute-start | bytes 1179656 | tf_op jit(solution)/shard_map/ppermute | solution.py:35
  212.6 20.9 %collective-permute-start.26 = (bf16[768,256]{1,0:T(8,128)(2,1)S(1)}, bf16[768,256]{1,0:T(8,128)(2,1)S(1)}, u32[]{:S(2)}, u32[]{:S(2)}) collective-permute-start(bf16[768,256]{1,0:T(8,128)(2,1)S(1)} %copy-done.38), channel_id=1, source_target_pairs={{0,8},{4,12},{8,0},{12,4},{16,24},{20,28},{24,16},{28,20},{1,9},{5... | collective-permute-start | bytes 1179656 | tf_op jit(solution)/shard_map/ppermute | solution.py:35
  212.6 20.9 %collective-permute-start.27 = (bf16[768,256]{1,0:T(8,128)(2,1)S(1)}, bf16[768,256]{1,0:T(8,128)(2,1)S(1)}, u32[]{:S(2)}, u32[]{:S(2)}) collective-permute-start(bf16[768,256]{1,0:T(8,128)(2,1)S(1)} %collective-permute-done.22), channel_id=1, source_target_pairs={{0,4},{4,0},{8,12},{12,8},{16,20},{20,16},{24,28},{28,24},{1,5},{5... | collective-permute-start | bytes 1179656 | tf_op jit(solution)/shard_map/ppermute | solution.py:35
  214.1 25.2 %collective-permute-start.32 = (bf16[768,256]{1,0:T(8,128)(2,1)S(1)}, bf16[768,256]{1,0:T(8,128)(2,1)S(1)}, u32[]{:S(2)}, u32[]{:S(2)}) collective-permute-start(bf16[768,256]{1,0:T(8,128)(2,1)S(1)} %copy-done.37), channel_id=1, source_target_pairs={{0,4},{4,0},{8,12},{12,8},{16,20},{20,16},{24,28},{28,24},{1,5},{5... | collective-permute-start | bytes 1179656 | tf_op jit(solution)/shard_map/ppermute | solution.py:35
  218.4 24.5 %collective-permute-start.33 = (bf16[768,256]{1,0:T(8,128)(2,1)S(1)}, bf16[768,256]{1,0:T(8,128)(2,1)S(1)}, u32[]{:S(2)}, u32[]{:S(2)}) collective-permute-start(bf16[768,256]{1,0:T(8,128)(2,1)S(1)} %convolution_convert_fusion.18), channel_id=1, source_target_pairs={{0,16},{4,20},{8,24},{12,28},{16,0},{20,4},{24,8},{28,12},{1,17},{... | collective-permute-start | bytes 1179656 | tf_op jit(solution)/shard_map/ppermute | solution.py:35
  235.1 21.9 %collective-permute-start.36 = (bf16[768,256]{1,0:T(8,128)(2,1)S(1)}, bf16[768,256]{1,0:T(8,128)(2,1)S(1)}, u32[]{:S(2)}, u32[]{:S(2)}) collective-permute-start(bf16[768,256]{1,0:T(8,128)(2,1)S(1)} %copy-done.36), channel_id=1, source_target_pairs={{0,4},{4,0},{8,12},{12,8},{16,20},{20,16},{24,28},{28,24},{1,5},{5... | collective-permute-start | bytes 1179656 | tf_op jit(solution)/shard_map/ppermute | solution.py:35
  252.6 22.3 %collective-permute-start.40 = (bf16[768,256]{1,0:T(8,128)(2,1)S(1)}, bf16[768,256]{1,0:T(8,128)(2,1)S(1)}, u32[]{:S(2)}, u32[]{:S(2)}) collective-permute-start(bf16[768,256]{1,0:T(8,128)(2,1)S(1)} %copy-done.35), channel_id=1, source_target_pairs={{0,4},{4,0},{8,12},{12,8},{16,20},{20,16},{24,28},{28,24},{1,5},{5... | collective-permute-start | bytes 1179656 | tf_op jit(solution)/shard_map/ppermute | solution.py:35
  270.6 21.9 %collective-permute-start.44 = (bf16[768,256]{1,0:T(8,128)(2,1)S(1)}, bf16[768,256]{1,0:T(8,128)(2,1)S(1)}, u32[]{:S(2)}, u32[]{:S(2)}) collective-permute-start(bf16[768,256]{1,0:T(8,128)(2,1)S(1)} %copy-done.34), channel_id=1, source_target_pairs={{0,4},{4,0},{8,12},{12,8},{16,20},{20,16},{24,28},{28,24},{1,5},{5... | collective-permute-start | bytes 1179656 | tf_op jit(solution)/shard_map/ppermute | solution.py:35
  288.2 23.3 %collective-permute-start.48 = (bf16[768,256]{1,0:T(8,128)(2,1)S(1)}, bf16[768,256]{1,0:T(8,128)(2,1)S(1)}, u32[]{:S(2)}, u32[]{:S(2)}) collective-permute-start(bf16[768,256]{1,0:T(8,128)(2,1)S(1)} %copy-done.33), channel_id=1, source_target_pairs={{0,4},{4,0},{8,12},{12,8},{16,20},{20,16},{24,28},{28,24},{1,5},{5... | collective-permute-start | bytes 1179656 | tf_op jit(solution)/shard_map/ppermute | solution.py:35
  292.5 19.9 %collective-permute-start.49 = (bf16[768,256]{1,0:T(8,128)(2,1)S(1)}, bf16[768,256]{1,0:T(8,128)(2,1)S(1)}, u32[]{:S(2)}, u32[]{:S(2)}) collective-permute-start(bf16[768,256]{1,0:T(8,128)(2,1)S(1)} %convolution_convert_fusion.14), channel_id=1, source_target_pairs={{0,16},{4,20},{8,24},{12,28},{16,0},{20,4},{24,8},{28,12},{1,17},{... | collective-permute-start | bytes 1179656 | tf_op jit(solution)/shard_map/ppermute | solution.py:35
  304.8 22.9 %collective-permute-start.52 = (bf16[768,256]{1,0:T(8,128)(2,1)S(1)}, bf16[768,256]{1,0:T(8,128)(2,1)S(1)}, u32[]{:S(2)}, u32[]{:S(2)}) collective-permute-start(bf16[768,256]{1,0:T(8,128)(2,1)S(1)} %copy-done.32), channel_id=1, source_target_pairs={{0,4},{4,0},{8,12},{12,8},{16,20},{20,16},{24,28},{28,24},{1,5},{5... | collective-permute-start | bytes 1179656 | tf_op jit(solution)/shard_map/ppermute | solution.py:35
  311.4 21.8 %collective-permute-start.53 = (bf16[768,256]{1,0:T(8,128)(2,1)S(1)}, bf16[768,256]{1,0:T(8,128)(2,1)S(1)}, u32[]{:S(2)}, u32[]{:S(2)}) collective-permute-start(bf16[768,256]{1,0:T(8,128)(2,1)S(1)} %convolution_convert_fusion.13), channel_id=1, source_target_pairs={{0,16},{4,20},{8,24},{12,28},{16,0},{20,4},{24,8},{28,12},{1,17},{... | collective-permute-start | bytes 1179656 | tf_op jit(solution)/shard_map/ppermute | solution.py:35
  321.0 22.4 %collective-permute-start.56 = (bf16[768,256]{1,0:T(8,128)(2,1)S(1)}, bf16[768,256]{1,0:T(8,128)(2,1)S(1)}, u32[]{:S(2)}, u32[]{:S(2)}) collective-permute-start(bf16[768,256]{1,0:T(8,128)(2,1)S(1)} %copy-done.31), channel_id=1, source_target_pairs={{0,4},{4,0},{8,12},{12,8},{16,20},{20,16},{24,28},{28,24},{1,5},{5... | collective-permute-start | bytes 1179656 | tf_op jit(solution)/shard_map/ppermute | solution.py:35
  327.8 22.8 %collective-permute-start.57 = (bf16[768,256]{1,0:T(8,128)(2,1)S(1)}, bf16[768,256]{1,0:T(8,128)(2,1)S(1)}, u32[]{:S(2)}, u32[]{:S(2)}) collective-permute-start(bf16[768,256]{1,0:T(8,128)(2,1)S(1)} %convolution_convert_fusion.12), channel_id=1, source_target_pairs={{0,16},{4,20},{8,24},{12,28},{16,0},{20,4},{24,8},{28,12},{1,17},{... | collective-permute-start | bytes 1179656 | tf_op jit(solution)/shard_map/ppermute | solution.py:35
  337.3 21.5 %collective-permute-start.60 = (bf16[768,256]{1,0:T(8,128)(2,1)S(1)}, bf16[768,256]{1,0:T(8,128)(2,1)S(1)}, u32[]{:S(2)}, u32[]{:S(2)}) collective-permute-start(bf16[768,256]{1,0:T(8,128)(2,1)S(1)} %copy-done.30), channel_id=1, source_target_pairs={{0,4},{4,0},{8,12},{12,8},{16,20},{20,16},{24,28},{28,24},{1,5},{5... | collective-permute-start | bytes 1179656 | tf_op jit(solution)/shard_map/ppermute | solution.py:35
  343.4 25.5 %collective-permute-start.61 = (bf16[768,256]{1,0:T(8,128)(2,1)S(1)}, bf16[768,256]{1,0:T(8,128)(2,1)S(1)}, u32[]{:S(2)}, u32[]{:S(2)}) collective-permute-start(bf16[768,256]{1,0:T(8,128)(2,1)S(1)} %convolution_convert_fusion.11), channel_id=1, source_target_pairs={{0,16},{4,20},{8,24},{12,28},{16,0},{20,4},{24,8},{28,12},{1,17},{... | collective-permute-start | bytes 1179656 | tf_op jit(solution)/shard_map/ppermute | solution.py:35
  352.4 24.8 %collective-permute-start.64 = (bf16[768,256]{1,0:T(8,128)(2,1)S(1)}, bf16[768,256]{1,0:T(8,128)(2,1)S(1)}, u32[]{:S(2)}, u32[]{:S(2)}) collective-permute-start(bf16[768,256]{1,0:T(8,128)(2,1)S(1)} %copy-done.29), channel_id=1, source_target_pairs={{0,4},{4,0},{8,12},{12,8},{16,20},{20,16},{24,28},{28,24},{1,5},{5... | collective-permute-start | bytes 1179656 | tf_op jit(solution)/shard_map/ppermute | solution.py:35
  358.8 21.4 %collective-permute-start.65 = (bf16[768,256]{1,0:T(8,128)(2,1)S(1)}, bf16[768,256]{1,0:T(8,128)(2,1)S(1)}, u32[]{:S(2)}, u32[]{:S(2)}) collective-permute-start(bf16[768,256]{1,0:T(8,128)(2,1)S(1)} %convolution_convert_fusion.10), channel_id=1, source_target_pairs={{0,16},{4,20},{8,24},{12,28},{16,0},{20,4},{24,8},{28,12},{1,17},{... | collective-permute-start | bytes 1179656 | tf_op jit(solution)/shard_map/ppermute | solution.py:35
  370.1 25.3 %collective-permute-start.68 = (bf16[768,256]{1,0:T(8,128)(2,1)S(1)}, bf16[768,256]{1,0:T(8,128)(2,1)S(1)}, u32[]{:S(2)}, u32[]{:S(2)}) collective-permute-start(bf16[768,256]{1,0:T(8,128)(2,1)S(1)} %copy-done.28), channel_id=1, source_target_pairs={{0,4},{4,0},{8,12},{12,8},{16,20},{20,16},{24,28},{28,24},{1,5},{5... | collective-permute-start | bytes 1179656 | tf_op jit(solution)/shard_map/ppermute | solution.py:35
  387.2 27.6 %collective-permute-start.72 = (bf16[768,256]{1,0:T(8,128)(2,1)S(1)}, bf16[768,256]{1,0:T(8,128)(2,1)S(1)}, u32[]{:S(2)}, u32[]{:S(2)}) collective-permute-start(bf16[768,256]{1,0:T(8,128)(2,1)S(1)} %copy-done.27), channel_id=1, source_target_pairs={{0,4},{4,0},{8,12},{12,8},{16,20},{20,16},{24,28},{28,24},{1,5},{5... | collective-permute-start | bytes 1179656 | tf_op jit(solution)/shard_map/ppermute | solution.py:35
  406.7 26.3 %collective-permute-start.76 = (bf16[768,256]{1,0:T(8,128)(2,1)S(1)}, bf16[768,256]{1,0:T(8,128)(2,1)S(1)}, u32[]{:S(2)}, u32[]{:S(2)}) collective-permute-start(bf16[768,256]{1,0:T(8,128)(2,1)S(1)} %copy-done.26), channel_id=1, source_target_pairs={{0,4},{4,0},{8,12},{12,8},{16,20},{20,16},{24,28},{28,24},{1,5},{5... | collective-permute-start | bytes 1179656 | tf_op jit(solution)/shard_map/ppermute | solution.py:35
  414.8 19.8 %collective-permute-start.77 = (bf16[768,256]{1,0:T(8,128)(2,1)S(1)}, bf16[768,256]{1,0:T(8,128)(2,1)S(1)}, u32[]{:S(2)}, u32[]{:S(2)}) collective-permute-start(bf16[768,256]{1,0:T(8,128)(2,1)S(1)} %convolution_convert_fusion.7), channel_id=1, source_target_pairs={{0,16},{4,20},{8,24},{12,28},{16,0},{20,4},{24,8},{28,12},{1,17},{... | collective-permute-start | bytes 1179656 | tf_op jit(solution)/shard_map/ppermute | solution.py:35
  425.6 25.6 %collective-permute-start.80 = (bf16[768,256]{1,0:T(8,128)(2,1)S(1)}, bf16[768,256]{1,0:T(8,128)(2,1)S(1)}, u32[]{:S(2)}, u32[]{:S(2)}) collective-permute-start(bf16[768,256]{1,0:T(8,128)(2,1)S(1)} %copy-done.25), channel_id=1, source_target_pairs={{0,4},{4,0},{8,12},{12,8},{16,20},{20,16},{24,28},{28,24},{1,5},{5... | collective-permute-start | bytes 1179656 | tf_op jit(solution)/shard_map/ppermute | solution.py:35
  433.0 20.7 %collective-permute-start.81 = (bf16[768,256]{1,0:T(8,128)(2,1)S(1)}, bf16[768,256]{1,0:T(8,128)(2,1)S(1)}, u32[]{:S(2)}, u32[]{:S(2)}) collective-permute-start(bf16[768,256]{1,0:T(8,128)(2,1)S(1)} %convolution_convert_fusion.6), channel_id=1, source_target_pairs={{0,16},{4,20},{8,24},{12,28},{16,0},{20,4},{24,8},{28,12},{1,17},{... | collective-permute-start | bytes 1179656 | tf_op jit(solution)/shard_map/ppermute | solution.py:35
  443.0 21.9 %collective-permute-start.84 = (bf16[768,256]{1,0:T(8,128)(2,1)S(1)}, bf16[768,256]{1,0:T(8,128)(2,1)S(1)}, u32[]{:S(2)}, u32[]{:S(2)}) collective-permute-start(bf16[768,256]{1,0:T(8,128)(2,1)S(1)} %copy-done.24), channel_id=1, source_target_pairs={{0,4},{4,0},{8,12},{12,8},{16,20},{20,16},{24,28},{28,24},{1,5},{5... | collective-permute-start | bytes 1179656 | tf_op jit(solution)/shard_map/ppermute | solution.py:35
  461.1 21.3 %collective-permute-start.88 = (bf16[768,256]{1,0:T(8,128)(2,1)S(1)}, bf16[768,256]{1,0:T(8,128)(2,1)S(1)}, u32[]{:S(2)}, u32[]{:S(2)}) collective-permute-start(bf16[768,256]{1,0:T(8,128)(2,1)S(1)} %copy-done.23), channel_id=1, source_target_pairs={{0,4},{4,0},{8,12},{12,8},{16,20},{20,16},{24,28},{28,24},{1,5},{5... | collective-permute-start | bytes 1179656 | tf_op jit(solution)/shard_map/ppermute | solution.py:35
  464.9 25.9 %collective-permute-start.89 = (bf16[768,256]{1,0:T(8,128)(2,1)S(1)}, bf16[768,256]{1,0:T(8,128)(2,1)S(1)}, u32[]{:S(2)}, u32[]{:S(2)}) collective-permute-start(bf16[768,256]{1,0:T(8,128)(2,1)S(1)} %convolution_convert_fusion.4), channel_id=1, source_target_pairs={{0,16},{4,20},{8,24},{12,28},{16,0},{20,4},{24,8},{28,12},{1,17},{... | collective-permute-start | bytes 1179656 | tf_op jit(solution)/shard_map/ppermute | solution.py:35
  478.5 28.6 %collective-permute-start.92 = (bf16[768,256]{1,0:T(8,128)(2,1)S(1)}, bf16[768,256]{1,0:T(8,128)(2,1)S(1)}, u32[]{:S(2)}, u32[]{:S(2)}) collective-permute-start(bf16[768,256]{1,0:T(8,128)(2,1)S(1)} %copy-done.22), channel_id=1, source_target_pairs={{0,4},{4,0},{8,12},{12,8},{16,20},{20,16},{24,28},{28,24},{1,5},{5... | collective-permute-start | bytes 1179656 | tf_op jit(solution)/shard_map/ppermute | solution.py:35
  482.4 39.2 %collective-permute-start.93 = (bf16[768,256]{1,0:T(8,128)(2,1)S(1)}, bf16[768,256]{1,0:T(8,128)(2,1)S(1)}, u32[]{:S(2)}, u32[]{:S(2)}) collective-permute-start(bf16[768,256]{1,0:T(8,128)(2,1)S(1)} %convolution_convert_fusion.3), channel_id=1, source_target_pairs={{0,16},{4,20},{8,24},{12,28},{16,0},{20,4},{24,8},{28,12},{1,17},{... | collective-permute-start | bytes 1179656 | tf_op jit(solution)/shard_map/ppermute | solution.py:35
  494.6 26.9 %collective-permute-start.90 = (bf16[768,256]{1,0:T(8,128)(2,1)S(1)}, bf16[768,256]{1,0:T(8,128)(2,1)S(1)}, u32[]{:S(2)}, u32[]{:S(2)}) collective-permute-start(bf16[768,256]{1,0:T(8,128)(2,1)S(1)} %copy-done.22), channel_id=1, source_target_pairs={{0,8},{4,12},{8,0},{12,4},{16,24},{20,28},{24,16},{28,20},{1,9},{5... | collective-permute-start | bytes 1179656 | tf_op jit(solution)/shard_map/ppermute | solution.py:35
  494.6 26.9 %collective-permute-start.91 = (bf16[768,256]{1,0:T(8,128)(2,1)S(1)}, bf16[768,256]{1,0:T(8,128)(2,1)S(1)}, u32[]{:S(2)}, u32[]{:S(2)}) collective-permute-start(bf16[768,256]{1,0:T(8,128)(2,1)S(1)} %collective-permute-done.86), channel_id=1, source_target_pairs={{0,4},{4,0},{8,12},{12,8},{16,20},{20,16},{24,28},{28,24},{1,5},{5... | collective-permute-start | bytes 1179656 | tf_op jit(solution)/shard_map/ppermute | solution.py:35
  498.2 35.9 %collective-permute-start.95 = (bf16[768,256]{1,0:T(8,128)(2,1)S(1)}, bf16[768,256]{1,0:T(8,128)(2,1)S(1)}, u32[]{:S(2)}, u32[]{:S(2)}) collective-permute-start(bf16[768,256]{1,0:T(8,128)(2,1)S(1)} %convolution_convert_fusion.2), channel_id=1, source_target_pairs={{0,16},{4,20},{8,24},{12,28},{16,0},{20,4},{24,8},{28,12},{1,17},{... | collective-permute-start | bytes 1179656 | tf_op jit(solution)/shard_map/ppermute | solution.py:35
  523.3 21.1 %collective-permute-start.96 = (bf16[768,256]{1,0:T(8,128)(2,1)S(1)}, bf16[768,256]{1,0:T(8,128)(2,1)S(1)}, u32[]{:S(2)}, u32[]{:S(2)}) collective-permute-start(bf16[768,256]{1,0:T(8,128)(2,1)S(1)} %convolution_convert_fusion.1), channel_id=1, source_target_pairs={{0,16},{4,20},{8,24},{12,28},{16,0},{20,4},{24,8},{28,12},{1,17},{... | collective-permute-start | bytes 1179656 | tf_op jit(solution)/shard_map/ppermute | solution.py:35
  (102 other events, 1331.6 us)
Sparse Core Ops, SparseCore 0:
  39.3 38.2 all-gather.6
  79.1 37.4 all-gather.4
